TPU v7x, 128 devices: a whole 4x4x4 slice. The times are simulated.
128 devices in a mesh: fsdp: 8 (over z, x_lo), tp: 16 (over x_hi, y, core).
Axes of the slice: x: 4 (x_hi: 2, x_lo: 2; x = x_hi * 2 + x_lo), y: 4, z: 4, core: 2. Of those that a mesh axis runs over, the one named last changes fastest.
Arguments:
- weight: bfloat16 [16384, 26624], P('fsdp', 'tp')
- adapter_down_factor: bfloat16 [16384, 64], P(('fsdp', 'tp')), may hold values from -6 to 6
- adapter_up_factor: bfloat16 [64, 26624], P('fsdp', 'tp'), may hold values from -0.75 to 0.75
- magnitude: float32 [26624], P('tp'), may hold values from 100 to 1000
- training_column_block: int32 [16, 13], replicated, may hold values from 0 to 207, as said below
Outputs:
- merged: bfloat16 [16384, 26624], P('fsdp', 'tp')
Inputs may be any that keep to these rules, and one draw needn't show every extreme that they name: training_column_block lists every column block once. Owner r's s-th block is block p_s of training shard (r - q_s) mod the tp axis size, i.e. training_column_block[r, s] = ((r - q_s) mod tp) * 13 + p_s, where p is a permutation of the 13 local positions and q takes 13 distinct offsets; at most 1 block of one training shard go to one owner, and exactly 1 do for some pair.
All inputs are finite; a program needn't handle non-finite values.
Results may differ from a plain program's by a relative error of at most 0.005.
Values may be sent and summed in bfloat16 or wider, within the bound.
No kernel may reach another device: no remote copies, remote signals or barrier semaphores. Data moves between devices by JAX's collectives and lax.ppermute only.
A program may use at most 128 MiB of HBM per device.

v0:
```python
import jax
import jax.numpy as jnp
from jax import lax
from jax.sharding import PartitionSpec as P


def per_device(weight, adapter_down_factor, adapter_up_factor, magnitude, training_column_block):
    tp_count = lax.axis_size("tp")
    own_index = lax.axis_index("tp")
    row_count = weight.shape[0]
    col_count = weight.shape[1]
    per_shard = training_column_block.shape[1]
    width_block = col_count // per_shard
    slot_count = (per_shard + tp_count - 1) // tp_count
    down_factor_rows = lax.all_gather(adapter_down_factor, "tp", axis=0, tiled=True)
    up_factor_columns = lax.all_gather(adapter_up_factor, "fsdp", axis=0, tiled=True)
    low_rank_update = jnp.dot(
        down_factor_rows, up_factor_columns, preferred_element_type=jnp.float32
    )
    combined = (weight.astype(jnp.float32) + low_rank_update).astype(jnp.bfloat16)
    partial_sq = jnp.sum(jnp.square(combined.astype(jnp.float32)), axis=0)
    squares = lax.psum(partial_sq, "fsdp")
    col_scale = magnitude * lax.rsqrt(squares + 1e-06)
    source_shard = training_column_block // per_shard
    source_local = training_column_block % per_shard
    matches = (source_shard == own_index).astype(jnp.int32)
    order_rank = jnp.cumsum(matches, axis=1) - 1
    slot_ids = jnp.arange(slot_count, dtype=jnp.int32)
    chosen = matches[:, None, :] * (order_rank[:, None, :] == slot_ids[None, :, None]).astype(
        jnp.int32
    )
    picked = jnp.sum(chosen * source_local[:, None, :], axis=2).reshape(-1)
    mine_shard = lax.dynamic_index_in_dim(source_shard, own_index, 0, keepdims=False)
    same_shard = (mine_shard[:, None] == mine_shard[None, :]).astype(jnp.int32)
    positions = jnp.arange(per_shard, dtype=jnp.int32)
    earlier = (positions[:, None] >= positions[None, :]).astype(jnp.int32)
    arrive_rank = jnp.sum(same_shard * earlier, axis=1) - 1
    placed = mine_shard * slot_count + arrive_rank
    scaled = (combined.astype(jnp.float32) * col_scale[None, :]).astype(jnp.bfloat16)
    packed = jnp.take(scaled.reshape(row_count, per_shard, width_block), picked, axis=1)
    arrived = lax.all_to_all(packed, "tp", split_axis=1, concat_axis=1, tiled=True)
    merged = jnp.take(arrived, placed, axis=1).reshape(row_count, col_count)
    return merged


def solution(mesh):
    return jax.shard_map(
        per_device,
        mesh=mesh,
        in_specs=(P("fsdp", "tp"), P(("fsdp", "tp"), None), P("fsdp", "tp"), P("tp"), P()),
        out_specs=P("fsdp", "tp"),
        check_vma=False,
    )
```

profile of v0, /device:TPU:27, one launch (start us, length us, event | category | flops | bytes accessed | tf_op | source)
XLA Modules:
  0.0 270.7 jit_solution(34445520871609743)
XLA Ops:
  0.0 0.7 compare_convert_fusion
  0.7 0.2 reduce_window_sum.11
  0.9 0.8 add_select_fusion.1
  1.7 24.0 %all_gather.7 = bf16[64,1664]{1,0:T(8,128)(2,1)S(1)} all-gather(bf16[8,1664]{1,0:T(8,128)(2,1)} %param.7), channel_id=1, replica_groups=mesh['fsdp'=8,'tp'=16] {'fsdp'}, dimensions={0}, use_global_device_ids=true | all-gather | bytes 239616 | tf_op jit(solution)/shard_map/all_gather | solution.py:16
  25.7 25.8 %all_gather.6 = bf16[2048,64]{0,1:T(8,128)(2,1)S(1)} all-gather(bf16[128,64]{0,1:T(8,128)(2,1)} %param.6), channel_id=1, replica_groups=mesh['fsdp'=8,'tp'=16] {'tp'}, dimensions={0}, use_global_device_ids=true | all-gather | bytes 278528 | tf_op jit(solution)/shard_map/all_gather | solution.py:15
  51.5 10.2 %copy.10 = bf16[2048,1664]{0,1:T(8,128)(2,1)} copy(bf16[2048,1664]{1,0:T(8,128)(2,1)} %param.5) | data formatting | bytes 13631488 | tf_op args[0]
  61.8 0.0 copy-start
  61.8 6.5 %fusion = (f32[1664]{0:T(1024)S(1)}, bf16[2048,1664]{0,1:T(8,128)(2,1)}) fusion(bf16[2048,64]{0,1:T(8,128)(2,1)S(1)} %all_gather.6, bf16[64,1664]{1,0:T(8,128)(2,1)S(1)} %all_gather.7, bf16[2048,1664]{0,1:T(8,128)(2,1)} %copy.10), kind=kOutput, calls=%fused_computation.4 | convolution fusion | flops 456653184 | bytes 14113280 | tf_op jit(solution)/shard_map/dot_general | solution.py:17
  68.2 13.2 %psum.7 = f32[1664]{0:T(1024)S(1)} all-reduce(f32[1664]{0:T(1024)S(1)} %get-tuple-element.7), channel_id=1, replica_groups=mesh['fsdp'=8,'tp'=16] {'fsdp'}, use_global_device_ids=true, to_apply=%region_4.5 | all-reduce | flops 1664 | bytes 13312 | tf_op jit(solution)/shard_map/psum | solution.py:22
  81.4 0.0 copy-done
  81.4 7.0 %fusion.1 = bf16[2048,1664]{0,1:T(8,128)(2,1)} fusion(bf16[2048,1664]{0,1:T(8,128)(2,1)} %get-tuple-element.8, f32[1664]{0:T(1024)S(1)} %rsqrt_multiply_fusion), kind=kLoop, calls=%fused_computation.5 | loop fusion | flops 10223616 | bytes 13638144 | tf_op jit(solution)/shard_map/convert_element_type | solution.py:39
  88.4 7.7 %gather_fusion = bf16[16,2048,128]{1,2,0:T(8,128)(2,1)} fusion(bf16[2048,13,128]{0,2,1:T(8,128)(2,1)} %bitcast.27, s32[1024]{0:T(1024)S(1)} %pad_clamp_fusion.1), kind=kCustom, calls=%fused_computation | custom fusion | bytes 16777280 | tf_op jit(solution)/shard_map/jit(_take)/gather | solution.py:40
  96.1 7.5 %select_bitcast_fusion = bf16[2048,16,128]{0,2,1:T(8,128)(2,1)} fusion(bf16[16,2048,128]{1,2,0:T(8,128)(2,1)} %gather_fusion, pred[16]{0:T(512)(128)(4,1)S(1)} %compare_and_fusion), kind=kLoop, calls=%fused_computation.7 | loop fusion | flops 4194304 | bytes 16777232 | tf_op jit(solution)/shard_map/jit(_take)/select_n | solution.py:40
  103.5 14.3 %all-to-all-start = ((bf16[2048,16,128]{0,2,1:T(8,128)(2,1)}), bf16[2048,16,128]{0,2,1:T(8,128)(2,1)}, u32[]{:S(2)}, u32[]{:S(2)}) async-start(bf16[2048,16,128]{0,2,1:T(8,128)(2,1)} %select_bitcast_fusion), calls=%async_computation | async-start | bytes 16777216 | tf_op jit(solution)/shard_map/all_to_all | solution.py:41
  117.8 0.2 select_reduce_fusion
  118.1 0.1 broadcast_bitcast_fusion
  118.2 128.7 %all-to-all-done = bf16[2048,16,128]{0,2,1:T(8,128)(2,1)} async-done(((bf16[2048,16,128]{0,2,1:T(8,128)(2,1)}), bf16[2048,16,128]{0,2,1:T(8,128)(2,1)}, u32[]{:S(2)}, u32[]{:S(2)}) %all-to-all-start) | async-done | bytes 8388640 | tf_op jit(solution)/shard_map/all_to_all | solution.py:41
  246.9 7.8 %gather_fusion.1 = bf16[13,2048,128]{1,2,0:T(8,128)(2,1)} fusion(bf16[2048,16,128]{0,2,1:T(8,128)(2,1)} %all-to-all-done, s32[1024]{0:T(1024)S(1)} %pad_clamp_fusion), kind=kCustom, calls=%fused_computation.1 | custom fusion | bytes 13631540 | tf_op jit(solution)/shard_map/jit(_take)/gather | solution.py:42
  254.7 6.4 %bitcast_select_fusion = bf16[2048,1664]{0,1:T(8,128)(2,1)} fusion(bf16[13,2048,128]{1,2,0:T(8,128)(2,1)} %gather_fusion.1, pred[1664]{0:T(1024)(128)(4,1)S(1)} %broadcast_bitcast_fusion), kind=kLoop, calls=%fused_computation.8 | loop fusion | flops 3407872 | bytes 13633152 | tf_op jit(solution)/shard_map/jit(_take)/select_n | solution.py:42
  261.1 9.7 %copy.11 = bf16[2048,1664]{1,0:T(8,128)(2,1)} copy(bf16[2048,1664]{0,1:T(8,128)(2,1)} %bitcast_select_fusion) | data formatting | bytes 13631488 | tf_op jit(solution)/shard_map/jit(_take)/select_n | solution.py:42
  (8 shorter events, 0.1 us)
Async XLA Ops:
  61.8 19.6 %copy-start = (f32[1664]{0:T(1024)S(1)}, f32[1664]{0:T(1024)}, u32[]{:S(2)}) copy-start(f32[1664]{0:T(1024)} %param.8) | copy-start | bytes 19972
  103.5 143.3 %all-to-all-start = ((bf16[2048,16,128]{0,2,1:T(8,128)(2,1)}), bf16[2048,16,128]{0,2,1:T(8,128)(2,1)}, u32[]{:S(2)}, u32[]{:S(2)}) async-start(bf16[2048,16,128]{0,2,1:T(8,128)(2,1)} %select_bitcast_fusion), calls=%async_computation | async-start | bytes 16777216 | tf_op jit(solution)/shard_map/all_to_all | solution.py:41
where the time goes:
time: 272 us; the launch traced here: 271 us
  waiting for transfers between devices  129 us (47%)
  blocking collectives  63 us (23%)
  local copies, waits for them, and re-layouts  35.4 us (13%)
  other arithmetic  22.8 us (8%)
  starting transfers between devices  14.3 us (5%)
  matrix products  6.46 us (2%)
    all_to_all x1, waiting for transfers between devices, per_device(): lax.all_to_all(packed, 'tp', split_axis=1, concat_axis=1, tiled=True)  129 us
    all_gather x1, blocking collectives, per_device(): lax.all_gather(adapter_down_factor, 'tp', axis=0, tiled=True)  25.8 us
    all_gather x1, blocking collectives, per_device(): lax.all_gather(adapter_up_factor, 'fsdp', axis=0, tiled=True)  24 us
    all_to_all x1, starting transfers between devices, per_device(): lax.all_to_all(packed, 'tp', split_axis=1, concat_axis=1, tiled=True)  14.3 us
    psum x1, blocking collectives, per_device(): squares = lax.psum(partial_sq, 'fsdp')  13.2 us
    unnamed x3, local copies, waits for them, and re-layouts  10.2 us
    select_n x1, local copies, waits for them, and re-layouts, per_device(): merged = jnp.take(arrived, placed, axis=1).reshape(row_count, col_count)  9.65 us
    gather x1, local copies, waits for them, and re-layouts, per_device(): merged = jnp.take(arrived, placed, axis=1).reshape(row_count, col_count)  7.79 us
  transfers between devices with their start and end apart: 1, of which 1 were waited for; matrix products, arithmetic and copies ran while one was open for 0% of the time, Pallas kernels for 0%

commit v1 on v0

v1 whole, which is shorter than its diff:
```python
import functools

import jax
import jax.numpy as jnp
from jax import lax
from jax.experimental import pallas as pl
from jax.experimental.pallas import tpu as pltpu
from jax.sharding import PartitionSpec as P

AXES = ("fsdp", "tp")
BLK = 128
SCALE_ROWS = 16
EXTRA = 80
OWN = (0, 0)
A_MASKS = (2, 6, 8, 1)
B_MASKS = (1, 2, 6)
BF16, F32 = jnp.bfloat16, jnp.float32
HBM = pl.BlockSpec(memory_space=pltpu.HBM)
ANY = pl.BlockSpec(memory_space=pl.ANY)
SMEM = pl.BlockSpec(memory_space=pltpu.SMEM)
VMEM = pl.BlockSpec(memory_space=pltpu.VMEM)


def shift_to(t, offset, flip):
    hi, y, core = t // 8, (t // 2) % 4, t % 2
    return ((hi + offset[0]) % 2) * 8 + ((y + offset[1]) % 4) * 2 + (core + flip) % 2


def tp_perm(offset, flip=0):
    return [(f * 16 + t, f * 16 + shift_to(t, offset, flip)) for f in range(8) for t in range(16)]


def tp_xor(mask):
    return [(f * 16 + t, f * 16 + (t ^ mask)) for f in range(8) for t in range(16)]


def fsdp_xor(mask):
    return [(f * 16 + t, (f ^ mask) * 16 + t) for f in range(8) for t in range(16)]


def send(x, perm):
    return lax.ppermute(x, AXES, perm)


def fill_tables(tcb, t, block_to, column_from):
    for i in range(16):
        block_to[i] = 0
        column_from[i] = -1
    for s in range(tcb.shape[1]):
        value = tcb[0, s]
        shard = value // tcb.shape[1]
        shift = (16 - shard) % 16
        block_to[(t + shift) % 16] = value - shard * tcb.shape[1]
        column_from[(t + 16 - shift) % 16] = s


def params(limit_mib, **kw):
    return pltpu.CompilerParams(vmem_limit_bytes=limit_mib << 20, **kw)


def columns(j):
    return pl.ds(pl.multiple_of(j * BLK, BLK), BLK)


def both(offset):
    return ((offset, 0), (offset, 1))


def pack_kernel(messages, tcb, w, *refs):
    outs, (buf, block_to, column_from, in_sems, out_sems) = refs[: len(messages)], refs[len(messages) :]
    t = lax.axis_index("tp")
    fill_tables(tcb, t, block_to, column_from)
    copies = []
    for out, message in zip(outs, messages):
        for n, (offset, flip) in enumerate(message):
            i, j = len(copies), block_to[shift_to(t, offset, flip)]
            copies.append(
                (
                    pltpu.make_async_copy(w.at[:, columns(j)], buf.at[i], in_sems.at[i]),
                    pltpu.make_async_copy(buf.at[i], out.at[n], out_sems.at[i]),
                )
            )
    for fetch, _ in copies:
        fetch.start()
    for fetch, store in copies:
        fetch.wait()
        store.start()
    for _, store in copies:
        store.wait()


def pack(tcb, w, messages):
    rows, count = w.shape[0], sum(len(m) for m in messages)
    return pl.pallas_call(
        functools.partial(pack_kernel, messages),
        out_shape=[jax.ShapeDtypeStruct((len(m), rows, BLK), BF16) for m in messages],
        in_specs=[SMEM, HBM],
        out_specs=[HBM] * len(messages),
        scratch_shapes=[
            pltpu.VMEM((count, rows, BLK), BF16),
            pltpu.SMEM((16,), jnp.int32),
            pltpu.SMEM((16,), jnp.int32),
            pltpu.SemaphoreType.DMA((count,)),
            pltpu.SemaphoreType.DMA((count,)),
        ],
        compiler_params=params(60),
        cost_estimate=pl.CostEstimate(flops=0, bytes_accessed=count * 4 * rows * BLK, transcendentals=0),
        name="pack",
    )(tcb, w)


def squares_kernel(w_hbm, a_rel, b_rel, sq, a_ord, b_ord, w, sems):
    t, f = lax.axis_index("tp"), lax.axis_index("fsdp")
    count, tile, width = w.shape
    fetches = [
        pltpu.make_async_copy(w_hbm.at[pl.ds(i * tile, tile)], w.at[i], sems.at[i]) for i in range(count)
    ]
    for c in fetches:
        c.start()
    row = lax.broadcasted_iota(jnp.int32, (64, 64), 0)
    col = lax.broadcasted_iota(jnp.int32, (64, 64), 1)
    slot = col >> 3
    shard = (slot ^ ((slot >> 1) & 2)) ^ f
    place = jnp.where(row == shard * 8 + (col & 7), 1.0, 0.0).astype(BF16)
    b_ord[...] = jnp.dot(place, b_rel[...], preferred_element_type=F32).astype(BF16)
    for i in range(16):
        rel = i ^ t
        r0, r1, r2, r3 = rel & 1, (rel >> 1) & 1, (rel >> 2) & 1, (rel >> 3) & 1
        slot = (r1 ^ r2) | (r2 << 1) | (r3 << 2) | (r0 << 3)
        a_ord[i * 128 : (i + 1) * 128, :] = a_rel[:, columns(slot)].astype(F32).T.astype(BF16)
    sums = [jnp.zeros((8, min(256, width - lo)), F32) for lo in range(0, width, 256)]
    for i in range(count):
        fetches[i].wait()
        a = a_ord[i * tile : (i + 1) * tile, :]
        for n, lo in enumerate(range(0, width, 256)):
            hi = min(lo + 256, width)
            low_rank = jnp.dot(a, b_ord[:, lo:hi], preferred_element_type=F32)
            combined = (w[i, :, lo:hi].astype(F32) + low_rank).astype(BF16).astype(F32)
            sums[n] += jnp.sum((combined * combined).reshape(tile // 8, 8, hi - lo), axis=0)
    for n, lo in enumerate(range(0, width, 256)):
        sq[:, lo : min(lo + 256, width)] = jnp.sum(sums[n], axis=0, keepdims=True)


def squares(w, a_rel, b_rel, tile=256):
    rows, width = w.shape
    return pl.pallas_call(
        squares_kernel,
        out_shape=[
            jax.ShapeDtypeStruct((1, width), F32),
            jax.ShapeDtypeStruct((rows, 64), BF16),
            jax.ShapeDtypeStruct((64, width), BF16),
        ],
        in_specs=[HBM, VMEM, VMEM],
        out_specs=[VMEM] * 3,
        scratch_shapes=[
            pltpu.VMEM((rows // tile, tile, width), BF16),
            pltpu.SemaphoreType.DMA((rows // tile,)),
        ],
        compiler_params=params(60),
        cost_estimate=pl.CostEstimate(flops=2 * rows * width * 64, bytes_accessed=2 * rows * width, transcendentals=0),
        name="column_squares",
    )(w, a_rel, b_rel)


def extras_kernel(tcb, b, sq, mag, out, buf, block_to, column_from, sems):
    fill_tables(tcb, lax.axis_index("tp"), block_to, column_from)
    scale = mag[...] * lax.rsqrt(sq[...] + 1e-06)
    row = lax.broadcasted_iota(jnp.int32, (SCALE_ROWS, BLK), 0)
    for j in range(buf.shape[0]):
        cols = slice(j * BLK, (j + 1) * BLK)
        s = scale[:, cols]
        high = s.astype(BF16).astype(F32)
        mid = (s - high).astype(BF16).astype(F32)
        low = s - high - mid
        parts = jnp.where(row == 0, high, jnp.where(row == 1, mid, jnp.where(row == 2, low, 0.0)))
        buf[j, 0:SCALE_ROWS, :] = parts.astype(BF16)
        buf[j, SCALE_ROWS:EXTRA, :] = b[:, cols]
    copies = [pltpu.make_async_copy(buf.at[block_to[r]], out.at[r], sems.at[r]) for r in range(16)]
    for c in copies:
        c.start()
    for c in copies:
        c.wait()


def pack_extras(tcb, b, sq, mag):
    per_shard = tcb.shape[1]
    return pl.pallas_call(
        extras_kernel,
        out_shape=jax.ShapeDtypeStruct((16, EXTRA, BLK), BF16),
        in_specs=[SMEM, VMEM, VMEM, VMEM],
        out_specs=HBM,
        scratch_shapes=[
            pltpu.VMEM((per_shard, EXTRA, BLK), BF16),
            pltpu.SMEM((16,), jnp.int32),
            pltpu.SMEM((16,), jnp.int32),
            pltpu.SemaphoreType.DMA((16,)),
        ],
        compiler_params=params(60),
        name="pack_extras",
    )(tcb, b, sq, mag)


def finish_kernel(blocks, first, tcb, a, extras, *refs):
    n = len(blocks)
    arrived, refs = refs[:n], refs[n if first else n + 1 :]
    out, raw, extra, done, block_to, column_from, raw_sems, extra_sems, done_sems = refs
    t = lax.axis_index("tp")
    fill_tables(tcb, t, block_to, column_from)
    here, fetches, stores = [], [], []
    for u, ((dx, dy), flip, at) in enumerate(blocks):
        shard = shift_to(t, (dx, (4 - dy) % 4), flip)
        column = column_from[shard]
        here.append(column >= 0)
        fetches.append(
            (
                pltpu.make_async_copy(extras.at[shard], extra.at[u], extra_sems.at[u]),
                pltpu.make_async_copy(arrived[u].at[at], raw.at[u], raw_sems.at[u]),
            )
        )
        target = out.at[:, columns(jnp.maximum(column, 0))]
        stores.append(pltpu.make_async_copy(done.at[u], target, done_sems.at[u]))
    for pair in fetches:
        for c in pair:
            c.start()
    for u in range(n):
        for c in fetches[u]:
            c.wait()

        @pl.when(here[u])
        def _():
            parts = extra[u, 0:SCALE_ROWS, :].astype(F32)
            scale = parts[0:1] + parts[1:2] + parts[2:3]
            b = extra[u, SCALE_ROWS:EXTRA, :]
            for lo in range(0, a.shape[0], 256):
                rows = slice(lo, lo + 256)
                low_rank = jnp.dot(a[rows, :], b, preferred_element_type=F32)
                combined = (raw[u, rows, :].astype(F32) + low_rank).astype(BF16).astype(F32)
                done[u, rows, :] = (combined * scale).astype(BF16)
            stores[u].start()

    for u in range(n):
        pl.when(here[u])(stores[u].wait)


def finish(tcb, a, extras, blocks, merged=None, width=None):
    rows, n, first = a.shape[0], len(blocks), merged is None
    arrays = [block[2] for block in blocks] + ([] if first else [merged])
    width = width if first else merged.shape[1]
    return pl.pallas_call(
        functools.partial(finish_kernel, [(block[0], block[1], block[3]) for block in blocks], first),
        out_shape=jax.ShapeDtypeStruct((rows, width), BF16),
        in_specs=[SMEM, VMEM, HBM] + [HBM] * len(arrays),
        out_specs=HBM,
        input_output_aliases={} if first else {3 + n: 0},
        scratch_shapes=[
            pltpu.VMEM((n, rows, BLK), BF16),
            pltpu.VMEM((n, EXTRA, BLK), BF16),
            pltpu.VMEM((n, rows, BLK), BF16),
            pltpu.SMEM((16,), jnp.int32),
            pltpu.SMEM((16,), jnp.int32),
            pltpu.SemaphoreType.DMA((n,)),
            pltpu.SemaphoreType.DMA((n,)),
            pltpu.SemaphoreType.DMA((n,)),
        ],
        compiler_params=params(60),
        cost_estimate=pl.CostEstimate(
            flops=2 * n * rows * BLK * 64, bytes_accessed=4 * n * rows * BLK, transcendentals=0
        ),
        name="finish",
    )(tcb, a, extras, *arrays)


def per_device(weight, adapter_down_factor, adapter_up_factor, magnitude, training_column_block):
    tcb = training_column_block
    after = lax.optimization_barrier
    chips = ((1, 0), (0, 1), (0, 3), (1, 2))
    singles = [(o, flip) for flip in range(2) for o in ((1, 1), (1, 3), (0, 2))]
    head = list(pack(tcb, weight, [both(o) for o in chips[:3]]))
    a, b = adapter_down_factor.T, adapter_up_factor
    a = jnp.concatenate([a, send(a, tp_xor(A_MASKS[0]))], axis=1)
    b = jnp.concatenate([b, send(b, fsdp_xor(B_MASKS[0]))], axis=0)
    a, b, head = after((a, b, head))
    direct = [None] * 4
    for n in (1, 2):
        direct[n] = send(head[n], tp_perm(chips[n]))
    for mask in A_MASKS[1:3]:
        a = jnp.concatenate([a, send(a, tp_xor(mask))], axis=1)
    a, head[0], weight_then = after((a, head[0], weight))
    direct[0] = send(head[0], tp_perm(chips[0]))
    a = jnp.concatenate([a, send(a, tp_xor(A_MASKS[3]))], axis=1)
    for mask in B_MASKS[1:]:
        b = jnp.concatenate([b, send(b, fsdp_xor(mask))], axis=0)
    sq, a, b = squares(weight, a, b)
    fourth, own, *single = pack(tcb, weight_then, [both(chips[3]), both(OWN)] + [(x,) for x in singles])
    sq = sq + send(sq, fsdp_xor(1))
    sq, direct[:3], fourth = after((sq, direct[:3], fourth))
    direct[3] = send(fourth, tp_perm(chips[3]))
    for mask in (2, 6):
        sq = sq + send(sq, fsdp_xor(mask))
    extras = pack_extras(tcb, b, sq, magnitude[None, :])
    extras = lax.all_to_all(extras, "tp", split_axis=0, concat_axis=0, tiled=True)
    extras, direct[3], single, own = after((extras, direct[3], single, own))
    single = [send(m, tp_perm(*x)) for m, x in zip(single, singles)]
    blocks = [(OWN, 0, own, 0), (OWN, 1, send(own, tp_xor(1)), 1)]
    for o, m in zip(chips, direct):
        blocks += [(o, 0, m, 0), (o, 1, send(m, tp_xor(1)), 1)]
    merged = finish(tcb, a, extras, blocks, width=weight.shape[1])
    merged = finish(tcb, a, extras, [(*x, m, 0) for x, m in zip(singles[:3], single[:3])], merged)
    return finish(tcb, a, extras, [(*x, m, 0) for x, m in zip(singles[3:], single[3:])], merged)


def solution(mesh):
    return jax.shard_map(
        per_device,
        mesh=mesh,
        in_specs=(P("fsdp", "tp"), P(("fsdp", "tp"), None), P("fsdp", "tp"), P("tp"), P()),
        out_specs=P("fsdp", "tp"),
        check_vma=False,
    )
```

time: 272 us -> 135 us (0.50)
  waiting for transfers between devices: 129 us -> 51.8 us
  blocking collectives: 63 us -> 0 us
  local copies, waits for them, and re-layouts: 35.4 us -> 0.64 us
  Pallas kernels: 0 us -> 32.6 us
  starting transfers between devices: 14.3 us -> 46.7 us
  other arithmetic: 22.8 us -> 2.07 us
  matrix products: 6.46 us -> 0 us
    all_to_all x1, waiting for transfers between devices: 129 us -> 10.2 us  [per_device(): lax.all_to_all(extras, 'tp', split_axis=0, concat_axis=0, tiled=True)]
    all_gather x2 -> x0, blocking collectives: 49.8 us -> none  [the longest x1 25.8 us: per_device(): lax.all_gather(adapter_down_factor, 'tp', axis=0, tiled=True)]
    ppermute x0 -> x25, waiting for transfers between devices: none -> 41.6 us  [send(): return lax.ppermute(x, AXES, perm)]
    ppermute x0 -> x25, starting transfers between devices: none -> 36.8 us  [send(): return lax.ppermute(x, AXES, perm)]
    pallas_call x0 -> x7, Pallas kernels: none -> 32.6 us  [the longest x3 13.9 us: finish(): pl.pallas_call(functools.partial(finish_kernel, [(block[0], block[1], blo...]
    gather x2 -> x0, local copies, waits for them, and re-layouts: 15.5 us -> none  [the longest x1 7.79 us: per_device(): merged = jnp.take(arrived, placed, axis=1).reshape(row_count, col_count)]
    select_n x5 -> x0, other arithmetic: 14.7 us -> none  [the longest x2 7.46 us: per_device(): jnp.take(scaled.reshape(row_count, per_shard, width_block), picked, axis=1)]
    psum x1 -> x0, blocking collectives: 13.2 us -> none  [per_device(): squares = lax.psum(partial_sq, 'fsdp')]
  transfers between devices with their start and end apart: 1 -> 26, of which waited for: 1 -> 12; matrix products, arithmetic and copies ran while one was open for 0% -> 2% of each run, Pallas kernels for 0% -> 21%
where the time goes in v1:
time: 135 us; the launch traced here: 134 us
  waiting for transfers between devices  51.8 us (38%)
  starting transfers between devices  46.7 us (35%)
  Pallas kernels  32.6 us (24%)
  other arithmetic  2.07 us (2%)
    ppermute x25, waiting for transfers between devices, send(): return lax.ppermute(x, AXES, perm)  41.6 us
    ppermute x25, starting transfers between devices, send(): return lax.ppermute(x, AXES, perm)  36.8 us
    pallas_call x3, Pallas kernels, finish(): pl.pallas_call(functools.partial(finish_kernel, [(block[0], block[1], blo...  13.9 us
    all_to_all x1, waiting for transfers between devices, per_device(): lax.all_to_all(extras, 'tp', split_axis=0, concat_axis=0, tiled=True)  10.2 us
    pallas_call x2, Pallas kernels, pack(): pl.pallas_call(functools.partial(pack_kernel, messages), out_shape=[jax.S...  10.1 us
    all_to_all x1, starting transfers between devices, per_device(): lax.all_to_all(extras, 'tp', split_axis=0, concat_axis=0, tiled=True)  9.82 us
    pallas_call x1, Pallas kernels, squares(): pl.pallas_call(squares_kernel, out_shape=[jax.ShapeDtypeStruct((1, width)...  6.54 us
  transfers between devices with their start and end apart: 26, of which 12 were waited for; matrix products, arithmetic and copies ran while one was open for 2% of the time, Pallas kernels for 21%

profile of v1, /device:TPU:27, one launch (start us, length us, event | category | flops | bytes accessed | tf_op | source)
XLA Modules:
  0.0 134.2 jit_solution(16407203681434624616)
XLA Ops:
  0.0 0.5 collective-permute-start
  0.5 0.3 collective-permute-start.1
  0.7 4.1 %pack.2 = (bf16[2,2048,128]{2,1,0:T(8,128)(2,1)}, bf16[2,2048,128]{2,1,0:T(8,128)(2,1)}, bf16[2,2048,128]{2,1,0:T(8,128)(2,1)}) custom-call(s32[16,13]{1,0:T(8,128)} %tcb.11, bf16[2048,1664]{1,0:T(8,128)(2,1)} %w.2), custom_call_target="tpu_custom_call" | custom-call | bytes 6291456 | tf_op jit(solution)/shard_map/pack/pallas_call | solution.py:94
  4.9 0.6 collective-permute-start.2
  5.5 3.5 %collective-permute-done.2 = bf16[64,256]{1,0:T(8,128)(2,1)S(1)} collective-permute-done((bf16[64,256]{1,0:T(8,128)(2,1)S(1)}, bf16[64,256]{1,0:T(8,128)(2,1)S(1)}, u32[]{:S(2)}, u32[]{:S(2)}) %collective-permute-start.2) | collective-permute-done | bytes 32800 | tf_op jit(solution)/shard_map/ppermute | solution.py:42
  9.0 2.1 %collective-permute-start.3 = (bf16[64,512]{1,0:T(8,128)(2,1)S(1)}, bf16[64,512]{1,0:T(8,128)(2,1)S(1)}, u32[]{:S(2)}, u32[]{:S(2)}) collective-permute-start(bf16[64,512]{1,0:T(8,128)(2,1)S(1)} %pad_maximum_fusion.4), channel_id=1, source_target_pairs={{0,8},{1,9},{2,10},{3,11},{4,12},{5,13},{6,14},{7,15},{8,0},{9,1},... | collective-permute-start | bytes 196616 | tf_op jit(solution)/shard_map/ppermute | solution.py:42
  11.1 0.5 collective-permute-start.9
  11.6 1.0 collective-permute-start.10
  12.6 1.0 collective-permute-done.3
  13.6 2.2 %collective-permute-start.8 = (bf16[2,2048,128]{2,1,0:T(8,128)(2,1)}, bf16[2,2048,128]{2,1,0:T(8,128)(2,1)S(1)}, u32[]{:S(2)}, u32[]{:S(2)}) collective-permute-start(bf16[2,2048,128]{2,1,0:T(8,128)(2,1)} %get-tuple-element.51), channel_id=1, source_target_pairs={{0,8},{1,9},{2,10},{3,11},{4,12},{5,13},{6,14},{7,15},{8,0},{9,1},... | collective-permute-start | bytes 3145736 | tf_op jit(solution)/shard_map/ppermute | solution.py:42
  15.9 1.6 %collective-permute-start.5 = (bf16[16,1664]{1,0:T(8,128)(2,1)S(1)}, bf16[16,1664]{1,0:T(8,128)(2,1)S(1)}, u32[]{:S(2)}, u32[]{:S(2)}) collective-permute-start(bf16[16,1664]{1,0:T(8,128)(2,1)S(1)} %pad_maximum_fusion.5), channel_id=1, source_target_pairs={{0,32},{1,33},{2,34},{3,35},{4,36},{5,37},{6,38},{7,39},{8,40},{9,... | collective-permute-start | bytes 159752 | tf_op jit(solution)/shard_map/ppermute | solution.py:42
  17.5 1.8 %collective-permute-done.5 = bf16[16,1664]{1,0:T(8,128)(2,1)S(1)} collective-permute-done((bf16[16,1664]{1,0:T(8,128)(2,1)S(1)}, bf16[16,1664]{1,0:T(8,128)(2,1)S(1)}, u32[]{:S(2)}, u32[]{:S(2)}) %collective-permute-start.5) | collective-permute-done | bytes 53280 | tf_op jit(solution)/shard_map/ppermute | solution.py:42
  19.3 3.7 %collective-permute-start.6 = (bf16[32,1664]{1,0:T(8,128)(2,1)S(1)}, bf16[32,1664]{1,0:T(8,128)(2,1)S(1)}, u32[]{:S(2)}, u32[]{:S(2)}) collective-permute-start(bf16[32,1664]{1,0:T(8,128)(2,1)S(1)} %pad_maximum_fusion.3), channel_id=1, source_target_pairs={{0,96},{1,97},{2,98},{3,99},{4,100},{5,101},{6,102},{7,103},{8,104... | collective-permute-start | bytes 319496 | tf_op jit(solution)/shard_map/ppermute | solution.py:42
  23.0 4.7 %collective-permute-start.4 = (bf16[64,1024]{1,0:T(8,128)(2,1)S(1)}, bf16[64,1024]{1,0:T(8,128)(2,1)S(1)}, u32[]{:S(2)}, u32[]{:S(2)}) collective-permute-start(bf16[64,1024]{1,0:T(8,128)(2,1)S(1)} %pad_maximum_fusion.2), channel_id=1, source_target_pairs={{0,1},{1,0},{2,3},{3,2},{4,5},{5,4},{6,7},{7,6},{8,9},{9,8},{10,11... | collective-permute-start | bytes 393224 | tf_op jit(solution)/shard_map/ppermute | solution.py:42
  27.7 0.7 pad_maximum_fusion.1.b_rel
  28.4 0.3 collective-permute-done.4
  28.7 0.7 pad_maximum_fusion.a_rel
  29.4 6.5 %column_squares.1 = (f32[1,1664]{1,0:T(1,128)}, bf16[2048,64]{1,0:T(8,128)(2,1)}, bf16[64,1664]{1,0:T(8,128)(2,1)}) custom-call(bf16[2048,1664]{1,0:T(8,128)(2,1)} %w.2, bf16[64,2048]{1,0:T(8,128)(2,1)} %pad_maximum_fusion.a_rel, bf16[64,1664]{1,0:T(8,128)(2,1)} %pad_maximum_fusion.1.b_rel), custom_call_target="tpu_custom_call" | custom-call | flops 436207616 | bytes 6815744 | tf_op jit(solution)/shard_map/column_squares/pallas_call | solution.py:146
  36.0 1.6 %collective-permute-start.7 = (f32[1,1664]{1,0:T(1,128)}, f32[1,1664]{1,0:T(1,128)S(1)}, u32[]{:S(2)}, u32[]{:S(2)}) collective-permute-start(f32[1,1664]{1,0:T(1,128)} %get-tuple-element.50), channel_id=1, source_target_pairs={{0,16},{1,17},{2,18},{3,19},{4,20},{5,21},{6,22},{7,23},{8,24},{9,... | collective-permute-start | bytes 19976 | tf_op jit(solution)/shard_map/ppermute | solution.py:42
  37.6 5.9 %pack.3 = (bf16[2,2048,128]{2,1,0:T(8,128)(2,1)}, bf16[2,2048,128]{2,1,0:T(8,128)(2,1)}, bf16[1,2048,128]{2,1,0:T(8,128)(2,1)}, bf16[1,2048,128]{2,1,0:T(8,128)(...) custom-call(s32[16,13]{1,0:T(8,128)} %tcb.11, ...), custom_call_target="tpu_custom_call" | custom-call | bytes 10485760 | tf_op jit(solution)/shard_map/pack/pallas_call | solution.py:94
  43.6 0.1 collective-permute-start.13
  43.7 2.8 %collective-permute-start.21 = (bf16[2,2048,128]{2,1,0:T(8,128)(2,1)S(1)}, bf16[2,2048,128]{2,1,0:T(8,128)(2,1)}, u32[]{:S(2)}, u32[]{:S(2)}) collective-permute-start(bf16[2,2048,128]{2,1,0:T(8,128)(2,1)S(1)} %collective-permute-done.8.refs_2_), channel_id=1, source_target_pairs={{0,1},{1,0},{2,3},{3,2},{4,5},{5,4},{6,7},{7,6},{8,9},{9,8},{10,11... | collective-permute-start | bytes 3145736 | tf_op jit(solution)/shard_map/ppermute | solution.py:42
  46.5 2.5 %collective-permute-done.11 = f32[1,1664]{1,0:T(1,128)S(1)} collective-permute-done((f32[1,1664]{1,0:T(1,128)S(1)}, f32[1,1664]{1,0:T(1,128)S(1)}, u32[]{:S(2)}, u32[]{:S(2)}) %collective-permute-start.11) | collective-permute-done | bytes 6688 | tf_op jit(solution)/shard_map/ppermute | solution.py:42
  49.0 3.0 %collective-permute-start.12 = (f32[1,1664]{1,0:T(1,128)S(1)}, f32[1,1664]{1,0:T(1,128)S(1)}, u32[]{:S(2)}, u32[]{:S(2)}) collective-permute-start(f32[1,1664]{1,0:T(1,128)S(1)} %add.10), channel_id=1, source_target_pairs={{0,96},{1,97},{2,98},{3,99},{4,100},{5,101},{6,102},{7,103},{8,104... | collective-permute-start | bytes 19976 | tf_op jit(solution)/shard_map/ppermute | solution.py:42
  52.0 0.6 broadcast_in_dim.3.mag
  52.6 0.4 collective-permute-done.12
  53.1 0.6 add.11.sq
  53.7 2.1 %pack_extras.1 = bf16[16,80,128]{2,1,0:T(8,128)(2,1)} custom-call(s32[16,13]{1,0:T(8,128)} %tcb.11, bf16[64,1664]{1,0:T(8,128)(2,1)} %get-tuple-element.49.b, f32[1,1664]{1,0:T(1,128)} %add.11.sq, f32[1,1664]{1,0:T(1,128)} %broadcast_in_dim.3.mag), custom_call_target="tpu_custom_call" | custom-call | tf_op jit(solution)/shard_map/pack_extras/pallas_call | solution.py:187
  55.8 9.8 %all-to-all-start = ((bf16[16,80,128]{2,1,0:T(8,128)(2,1)}), bf16[16,80,128]{2,1,0:T(8,128)(2,1)S(1)}, u32[]{:S(2)}, u32[]{:S(2)}) async-start(bf16[16,80,128]{2,1,0:T(8,128)(2,1)} %pack_extras.1), calls=%async_computation | async-start | bytes 655360 | tf_op jit(solution)/shard_map/all_to_all | solution.py:301
  65.6 0.4 collective-permute-start.22
  66.0 0.1 collective-permute-start.23
  66.1 10.2 %all-to-all-done.extras = bf16[16,80,128]{2,1,0:T(8,128)(2,1)S(1)} async-done(((bf16[16,80,128]{2,1,0:T(8,128)(2,1)}), bf16[16,80,128]{2,1,0:T(8,128)(2,1)S(1)}, u32[]{:S(2)}, u32[]{:S(2)}) %all-to-all-start) | async-done | bytes 327712 | tf_op jit(solution)/shard_map/all_to_all | solution.py:301
  76.3 0.4 collective-permute-start.20
  76.7 0.1 collective-permute-start.24
  76.8 0.7 collective-permute-start.17
  77.6 3.1 %collective-permute-start.18 = (bf16[1,2048,128]{2,1,0:T(8,128)(2,1)}, bf16[1,2048,128]{2,1,0:T(8,128)(2,1)}, u32[]{:S(2)}, u32[]{:S(2)}) collective-permute-start(bf16[1,2048,128]{2,1,0:T(8,128)(2,1)} %get-tuple-element.70), channel_id=1, source_target_pairs={{0,14},{1,15},{2,8},{3,9},{4,10},{5,11},{6,12},{7,13},{8,6},{9,7},... | collective-permute-start | bytes 1572872 | tf_op jit(solution)/shard_map/ppermute | solution.py:42
  80.7 0.7 collective-permute-start.19
  81.4 11.3 %collective-permute-done.17.refs_0_ = bf16[1,2048,128]{2,1,0:T(8,128)(2,1)S(1)} collective-permute-done((bf16[1,2048,128]{2,1,0:T(8,128)(2,1)}, bf16[1,2048,128]{2,1,0:T(8,128)(2,1)S(1)}, u32[]{:S(2)}, u32[]{:S(2)}) %collective-permute-start.17) | collective-permute-done | bytes 524320 | tf_op jit(solution)/shard_map/ppermute | solution.py:42
  92.7 3.8 %collective-permute-start.14 = (bf16[1,2048,128]{2,1,0:T(8,128)(2,1)}, bf16[1,2048,128]{2,1,0:T(8,128)(2,1)}, u32[]{:S(2)}, u32[]{:S(2)}) collective-permute-start(bf16[1,2048,128]{2,1,0:T(8,128)(2,1)} %get-tuple-element.66), channel_id=1, source_target_pairs={{0,11},{1,10},{2,13},{3,12},{4,15},{5,14},{6,9},{7,8},{8,3},{9,2},... | collective-permute-start | bytes 1572872 | tf_op jit(solution)/shard_map/ppermute | solution.py:42
  96.5 0.3 collective-permute-start.15
  96.9 2.5 %collective-permute-start.16 = (bf16[1,2048,128]{2,1,0:T(8,128)(2,1)}, bf16[1,2048,128]{2,1,0:T(8,128)(2,1)}, u32[]{:S(2)}, u32[]{:S(2)}) collective-permute-start(bf16[1,2048,128]{2,1,0:T(8,128)(2,1)} %get-tuple-element.68), channel_id=1, source_target_pairs={{0,5},{1,4},{2,7},{3,6},{4,1},{5,0},{6,3},{7,2},{8,13},{9,12},{10,... | collective-permute-start | bytes 1572872 | tf_op jit(solution)/shard_map/ppermute | solution.py:42
  99.4 5.8 %finish.3.refs_3_ = bf16[2048,1664]{1,0:T(8,128)(2,1)} custom-call(s32[16,13]{1,0:T(8,128)} %tcb.11, bf16[2048,64]{1,0:T(8,128)(2,1)} %get-tuple-element.48.a, bf16[16,80,128]{2,1,0:T(8,128)(2,1)} %copy-done, bf16[2,2048,128]{2,1,0:T(8,128)(2,1)} %get-tuple-element.72.refs_0_, bf16[2,2048,128]{2,1,0:T(8,128)(2,1)} %collective-permute-done.20.refs_1_, ...), custom_call_target="tpu_custom_call" | custom-call | flops 335544320 | bytes 10485760 | tf_op jit(solution)/shard_map/finish/pallas_call | solution.py:249
  105.3 1.0 collective-permute-done.19.refs_2_
  106.3 4.0 %finish.4.refs_3_ = bf16[2048,1664]{1,0:T(8,128)(2,1)} custom-call(s32[16,13]{1,0:T(8,128)} %tcb.11, bf16[2048,64]{1,0:T(8,128)(2,1)} %get-tuple-element.48.a, bf16[16,80,128]{2,1,0:T(8,128)(2,1)} %copy-done, bf16[1,2048,128]{2,1,0:T(8,128)(2,1)} %copy-done.4, bf16[1,2048,128]{2,1,0:T(8,128)(2,1)} %collective-permute-done.18.refs_1_, ...), custom_call_target="tpu_custom_call", output_to_operand_aliasing={{}: (6, {})} | custom-call | flops 100663296 | bytes 3145728 | tf_op jit(solution)/shard_map/finish/pallas_call | solution.py:249
  110.3 7.2 %collective-permute-done.14.refs_0_ = bf16[1,2048,128]{2,1,0:T(8,128)(2,1)} collective-permute-done((bf16[1,2048,128]{2,1,0:T(8,128)(2,1)}, bf16[1,2048,128]{2,1,0:T(8,128)(2,1)}, u32[]{:S(2)}, u32[]{:S(2)}) %collective-permute-start.14) | collective-permute-done | bytes 524320 | tf_op jit(solution)/shard_map/ppermute | solution.py:42
  117.5 10.9 %collective-permute-done.15.refs_1_ = bf16[1,2048,128]{2,1,0:T(8,128)(2,1)} collective-permute-done((bf16[1,2048,128]{2,1,0:T(8,128)(2,1)}, bf16[1,2048,128]{2,1,0:T(8,128)(2,1)}, u32[]{:S(2)}, u32[]{:S(2)}) %collective-permute-start.15) | collective-permute-done | bytes 524320 | tf_op jit(solution)/shard_map/ppermute | solution.py:42
  128.4 1.5 %collective-permute-done.16.refs_2_ = bf16[1,2048,128]{2,1,0:T(8,128)(2,1)} collective-permute-done((bf16[1,2048,128]{2,1,0:T(8,128)(2,1)}, bf16[1,2048,128]{2,1,0:T(8,128)(2,1)}, u32[]{:S(2)}, u32[]{:S(2)}) %collective-permute-start.16) | collective-permute-done | bytes 524320 | tf_op jit(solution)/shard_map/ppermute | solution.py:42
  129.9 4.1 %finish.5 = bf16[2048,1664]{1,0:T(8,128)(2,1)} custom-call(s32[16,13]{1,0:T(8,128)} %tcb.11, bf16[2048,64]{1,0:T(8,128)(2,1)} %get-tuple-element.48.a, bf16[16,80,128]{2,1,0:T(8,128)(2,1)} %copy-done, bf16[1,2048,128]{2,1,0:T(8,128)(2,1)} %collective-permute-done.14.refs_0_, ...), custom_call_target="tpu_custom_call", output_to_operand_aliasing={{}: (6, {})} | custom-call | flops 100663296 | bytes 3145728 | tf_op jit(solution)/shard_map/finish/pallas_call | solution.py:249
  (40 shorter events, 0.1 us)
Async XLA Ops:
  0.0 4.9 %copy-start.6 = (bf16[128,64]{0,1:T(8,128)(2,1)S(1)}, bf16[128,64]{0,1:T(8,128)(2,1)}, u32[]{:S(2)}) copy-start(bf16[128,64]{0,1:T(8,128)(2,1)} %param.6) | copy-start | bytes 49156
  0.0 4.9 %copy-start.5 = (bf16[8,1664]{1,0:T(8,128)(2,1)S(1)}, bf16[8,1664]{1,0:T(8,128)(2,1)}, u32[]{:S(2)}) copy-start(bf16[8,1664]{1,0:T(8,128)(2,1)} %param.7) | copy-start | bytes 79876
  0.0 4.9 %collective-permute-start = (bf16[64,128]{1,0:T(8,128)(2,1)}, bf16[64,128]{1,0:T(8,128)(2,1)S(1)}, u32[]{:S(2)}, u32[]{:S(2)}) collective-permute-start(bf16[64,128]{1,0:T(8,128)(2,1)} %bitcast.1), channel_id=1, source_target_pairs={{0,2},{1,3},{2,0},{3,1},{4,6},{5,7},{6,4},{7,5},{8,10},{9,11},{10,... | collective-permute-start | bytes 49160 | tf_op jit(solution)/shard_map/ppermute | solution.py:42
  0.5 4.4 %collective-permute-start.1 = (bf16[8,1664]{1,0:T(8,128)(2,1)}, bf16[8,1664]{1,0:T(8,128)(2,1)S(1)}, u32[]{:S(2)}, u32[]{:S(2)}) collective-permute-start(bf16[8,1664]{1,0:T(8,128)(2,1)} %param.7), channel_id=1, source_target_pairs={{0,16},{1,17},{2,18},{3,19},{4,20},{5,21},{6,22},{7,23},{8,24},{9,... | collective-permute-start | bytes 79880 | tf_op jit(solution)/shard_map/ppermute | solution.py:42
  4.9 4.1 %collective-permute-start.2 = (bf16[64,256]{1,0:T(8,128)(2,1)S(1)}, bf16[64,256]{1,0:T(8,128)(2,1)S(1)}, u32[]{:S(2)}, u32[]{:S(2)}) collective-permute-start(bf16[64,256]{1,0:T(8,128)(2,1)S(1)} %pad_maximum_fusion.6), channel_id=1, source_target_pairs={{0,6},{1,7},{2,4},{3,5},{4,2},{5,3},{6,0},{7,1},{8,14},{9,15},{10,... | collective-permute-start | bytes 98312 | tf_op jit(solution)/shard_map/ppermute | solution.py:42
  9.0 4.6 %collective-permute-start.3 = (bf16[64,512]{1,0:T(8,128)(2,1)S(1)}, bf16[64,512]{1,0:T(8,128)(2,1)S(1)}, u32[]{:S(2)}, u32[]{:S(2)}) collective-permute-start(bf16[64,512]{1,0:T(8,128)(2,1)S(1)} %pad_maximum_fusion.4), channel_id=1, source_target_pairs={{0,8},{1,9},{2,10},{3,11},{4,12},{5,13},{6,14},{7,15},{8,0},{9,1},... | collective-permute-start | bytes 196616 | tf_op jit(solution)/shard_map/ppermute | solution.py:42
  11.1 32.5 %collective-permute-start.9 = (bf16[2,2048,128]{2,1,0:T(8,128)(2,1)}, bf16[2,2048,128]{2,1,0:T(8,128)(2,1)S(1)}, u32[]{:S(2)}, u32[]{:S(2)}) collective-permute-start(bf16[2,2048,128]{2,1,0:T(8,128)(2,1)} %get-tuple-element.52), channel_id=1, source_target_pairs={{0,2},{1,3},{2,4},{3,5},{4,6},{5,7},{6,0},{7,1},{8,10},{9,11},{10,... | collective-permute-start | bytes 3145736 | tf_op jit(solution)/shard_map/ppermute | solution.py:42
  11.6 32.0 %collective-permute-start.10 = (bf16[2,2048,128]{2,1,0:T(8,128)(2,1)}, bf16[2,2048,128]{2,1,0:T(8,128)(2,1)S(1)}, u32[]{:S(2)}, u32[]{:S(2)}) collective-permute-start(bf16[2,2048,128]{2,1,0:T(8,128)(2,1)} %get-tuple-element.53), channel_id=1, source_target_pairs={{0,6},{1,7},{2,0},{3,1},{4,2},{5,3},{6,4},{7,5},{8,14},{9,15},{10,... | collective-permute-start | bytes 3145736 | tf_op jit(solution)/shard_map/ppermute | solution.py:42
  13.6 30.0 %collective-permute-start.8 = (bf16[2,2048,128]{2,1,0:T(8,128)(2,1)}, bf16[2,2048,128]{2,1,0:T(8,128)(2,1)S(1)}, u32[]{:S(2)}, u32[]{:S(2)}) collective-permute-start(bf16[2,2048,128]{2,1,0:T(8,128)(2,1)} %get-tuple-element.51), channel_id=1, source_target_pairs={{0,8},{1,9},{2,10},{3,11},{4,12},{5,13},{6,14},{7,15},{8,0},{9,1},... | collective-permute-start | bytes 3145736 | tf_op jit(solution)/shard_map/ppermute | solution.py:42
  15.9 3.5 %collective-permute-start.5 = (bf16[16,1664]{1,0:T(8,128)(2,1)S(1)}, bf16[16,1664]{1,0:T(8,128)(2,1)S(1)}, u32[]{:S(2)}, u32[]{:S(2)}) collective-permute-start(bf16[16,1664]{1,0:T(8,128)(2,1)S(1)} %pad_maximum_fusion.5), channel_id=1, source_target_pairs={{0,32},{1,33},{2,34},{3,35},{4,36},{5,37},{6,38},{7,39},{8,40},{9,... | collective-permute-start | bytes 159752 | tf_op jit(solution)/shard_map/ppermute | solution.py:42
  19.3 8.4 %collective-permute-start.6 = (bf16[32,1664]{1,0:T(8,128)(2,1)S(1)}, bf16[32,1664]{1,0:T(8,128)(2,1)S(1)}, u32[]{:S(2)}, u32[]{:S(2)}) collective-permute-start(bf16[32,1664]{1,0:T(8,128)(2,1)S(1)} %pad_maximum_fusion.3), channel_id=1, source_target_pairs={{0,96},{1,97},{2,98},{3,99},{4,100},{5,101},{6,102},{7,103},{8,104... | collective-permute-start | bytes 319496 | tf_op jit(solution)/shard_map/ppermute | solution.py:42
  23.0 5.7 %collective-permute-start.4 = (bf16[64,1024]{1,0:T(8,128)(2,1)S(1)}, bf16[64,1024]{1,0:T(8,128)(2,1)S(1)}, u32[]{:S(2)}, u32[]{:S(2)}) collective-permute-start(bf16[64,1024]{1,0:T(8,128)(2,1)S(1)} %pad_maximum_fusion.2), channel_id=1, source_target_pairs={{0,1},{1,0},{2,3},{3,2},{4,5},{5,4},{6,7},{7,6},{8,9},{9,8},{10,11... | collective-permute-start | bytes 393224 | tf_op jit(solution)/shard_map/ppermute | solution.py:42
  29.4 22.6 %copy-start.7 = (f32[1664]{0:T(1024)S(1)}, f32[1664]{0:T(1024)}, u32[]{:S(2)}) copy-start(f32[1664]{0:T(1024)} %param.8) | copy-start | bytes 19972
  36.0 7.6 %copy-start.8 = (f32[1,1664]{1,0:T(1,128)S(1)}, f32[1,1664]{1,0:T(1,128)}, u32[]{:S(2)}) copy-start(f32[1,1664]{1,0:T(1,128)} %get-tuple-element.50) | copy-start | bytes 19972
  36.0 7.6 %collective-permute-start.7 = (f32[1,1664]{1,0:T(1,128)}, f32[1,1664]{1,0:T(1,128)S(1)}, u32[]{:S(2)}, u32[]{:S(2)}) collective-permute-start(f32[1,1664]{1,0:T(1,128)} %get-tuple-element.50), channel_id=1, source_target_pairs={{0,16},{1,17},{2,18},{3,19},{4,20},{5,21},{6,22},{7,23},{8,24},{9,... | collective-permute-start | bytes 19976 | tf_op jit(solution)/shard_map/ppermute | solution.py:42
  43.6 55.8 %copy-start.1 = (bf16[2,2048,128]{2,1,0:T(8,128)(2,1)}, bf16[2,2048,128]{2,1,0:T(8,128)(2,1)S(1)}, u32[]{:S(2)}) copy-start(bf16[2,2048,128]{2,1,0:T(8,128)(2,1)S(1)} %collective-permute-done.9.refs_4_) | copy-start | bytes 3145732
  43.6 55.8 %copy-start.2 = (bf16[2,2048,128]{2,1,0:T(8,128)(2,1)}, bf16[2,2048,128]{2,1,0:T(8,128)(2,1)S(1)}, u32[]{:S(2)}) copy-start(bf16[2,2048,128]{2,1,0:T(8,128)(2,1)S(1)} %collective-permute-done.10.refs_6_) | copy-start | bytes 3145732
  43.6 55.8 %copy-start.3 = (bf16[2,2048,128]{2,1,0:T(8,128)(2,1)}, bf16[2,2048,128]{2,1,0:T(8,128)(2,1)S(1)}, u32[]{:S(2)}) copy-start(bf16[2,2048,128]{2,1,0:T(8,128)(2,1)S(1)} %collective-permute-done.8.refs_2_) | copy-start | bytes 3145732
  43.6 32.7 %collective-permute-start.13 = (bf16[2,2048,128]{2,1,0:T(8,128)(2,1)}, bf16[2,2048,128]{2,1,0:T(8,128)(2,1)}, u32[]{:S(2)}, u32[]{:S(2)}) collective-permute-start(bf16[2,2048,128]{2,1,0:T(8,128)(2,1)} %get-tuple-element.57), channel_id=1, source_target_pairs={{0,12},{1,13},{2,14},{3,15},{4,8},{5,9},{6,10},{7,11},{8,4},{9,5},... | collective-permute-start | bytes 3145736 | tf_op jit(solution)/shard_map/ppermute | solution.py:42
  43.7 33.1 %collective-permute-start.21 = (bf16[2,2048,128]{2,1,0:T(8,128)(2,1)S(1)}, bf16[2,2048,128]{2,1,0:T(8,128)(2,1)}, u32[]{:S(2)}, u32[]{:S(2)}) collective-permute-start(bf16[2,2048,128]{2,1,0:T(8,128)(2,1)S(1)} %collective-permute-done.8.refs_2_), channel_id=1, source_target_pairs={{0,1},{1,0},{2,3},{3,2},{4,5},{5,4},{6,7},{7,6},{8,9},{9,8},{10,11... | collective-permute-start | bytes 3145736 | tf_op jit(solution)/shard_map/ppermute | solution.py:42
  46.5 2.5 %collective-permute-start.11 = (f32[1,1664]{1,0:T(1,128)S(1)}, f32[1,1664]{1,0:T(1,128)S(1)}, u32[]{:S(2)}, u32[]{:S(2)}) collective-permute-start(f32[1,1664]{1,0:T(1,128)S(1)} %add.9), channel_id=1, source_target_pairs={{0,32},{1,33},{2,34},{3,35},{4,36},{5,37},{6,38},{7,39},{8,40},{9,... | collective-permute-start | bytes 19976 | tf_op jit(solution)/shard_map/ppermute | solution.py:42
  49.0 4.1 %collective-permute-start.12 = (f32[1,1664]{1,0:T(1,128)S(1)}, f32[1,1664]{1,0:T(1,128)S(1)}, u32[]{:S(2)}, u32[]{:S(2)}) collective-permute-start(f32[1,1664]{1,0:T(1,128)S(1)} %add.10), channel_id=1, source_target_pairs={{0,96},{1,97},{2,98},{3,99},{4,100},{5,101},{6,102},{7,103},{8,104... | collective-permute-start | bytes 19976 | tf_op jit(solution)/shard_map/ppermute | solution.py:42
  55.8 20.5 %all-to-all-start = ((bf16[16,80,128]{2,1,0:T(8,128)(2,1)}), bf16[16,80,128]{2,1,0:T(8,128)(2,1)S(1)}, u32[]{:S(2)}, u32[]{:S(2)}) async-start(bf16[16,80,128]{2,1,0:T(8,128)(2,1)} %pack_extras.1), calls=%async_computation | async-start | bytes 655360 | tf_op jit(solution)/shard_map/all_to_all | solution.py:301
  65.6 12.0 %collective-permute-start.22 = (bf16[2,2048,128]{2,1,0:T(8,128)(2,1)S(1)}, bf16[2,2048,128]{2,1,0:T(8,128)(2,1)}, u32[]{:S(2)}, u32[]{:S(2)}) collective-permute-start(bf16[2,2048,128]{2,1,0:T(8,128)(2,1)S(1)} %collective-permute-done.9.refs_4_), channel_id=1, source_target_pairs={{0,1},{1,0},{2,3},{3,2},{4,5},{5,4},{6,7},{7,6},{8,9},{9,8},{10,11... | collective-permute-start | bytes 3145736 | tf_op jit(solution)/shard_map/ppermute | solution.py:42
  66.0 14.8 %collective-permute-start.23 = (bf16[2,2048,128]{2,1,0:T(8,128)(2,1)S(1)}, bf16[2,2048,128]{2,1,0:T(8,128)(2,1)}, u32[]{:S(2)}, u32[]{:S(2)}) collective-permute-start(bf16[2,2048,128]{2,1,0:T(8,128)(2,1)S(1)} %collective-permute-done.10.refs_6_), channel_id=1, source_target_pairs={{0,1},{1,0},{2,3},{3,2},{4,5},{5,4},{6,7},{7,6},{8,9},{9,8},{10,11... | collective-permute-start | bytes 3145736 | tf_op jit(solution)/shard_map/ppermute | solution.py:42
  76.3 23.1 %copy-start = (bf16[16,80,128]{2,1,0:T(8,128)(2,1)}, bf16[16,80,128]{2,1,0:T(8,128)(2,1)S(1)}, u32[]{:S(2)}) copy-start(bf16[16,80,128]{2,1,0:T(8,128)(2,1)S(1)} %all-to-all-done.extras) | copy-start | bytes 983044
  76.3 20.2 %collective-permute-start.20 = (bf16[2,2048,128]{2,1,0:T(8,128)(2,1)}, bf16[2,2048,128]{2,1,0:T(8,128)(2,1)}, u32[]{:S(2)}, u32[]{:S(2)}) collective-permute-start(bf16[2,2048,128]{2,1,0:T(8,128)(2,1)} %get-tuple-element.72.refs_0_), channel_id=1, source_target_pairs={{0,1},{1,0},{2,3},{3,2},{4,5},{5,4},{6,7},{7,6},{8,9},{9,8},{10,11... | collective-permute-start | bytes 3145736 | tf_op jit(solution)/shard_map/ppermute | solution.py:42
  76.7 20.2 %collective-permute-start.24 = (bf16[2,2048,128]{2,1,0:T(8,128)(2,1)}, bf16[2,2048,128]{2,1,0:T(8,128)(2,1)}, u32[]{:S(2)}, u32[]{:S(2)}) collective-permute-start(bf16[2,2048,128]{2,1,0:T(8,128)(2,1)} %collective-permute-done.13.refs_8_), channel_id=1, source_target_pairs={{0,1},{1,0},{2,3},{3,2},{4,5},{5,4},{6,7},{7,6},{8,9},{9,8},{10,11... | collective-permute-start | bytes 3145736 | tf_op jit(solution)/shard_map/ppermute | solution.py:42
  76.8 15.9 %collective-permute-start.17 = (bf16[1,2048,128]{2,1,0:T(8,128)(2,1)}, bf16[1,2048,128]{2,1,0:T(8,128)(2,1)S(1)}, u32[]{:S(2)}, u32[]{:S(2)}) collective-permute-start(bf16[1,2048,128]{2,1,0:T(8,128)(2,1)} %get-tuple-element.69), channel_id=1, source_target_pairs={{0,10},{1,11},{2,12},{3,13},{4,14},{5,15},{6,8},{7,9},{8,2},{9,3},... | collective-permute-start | bytes 1572872 | tf_op jit(solution)/shard_map/ppermute | solution.py:42
  77.6 27.7 %collective-permute-start.18 = (bf16[1,2048,128]{2,1,0:T(8,128)(2,1)}, bf16[1,2048,128]{2,1,0:T(8,128)(2,1)}, u32[]{:S(2)}, u32[]{:S(2)}) collective-permute-start(bf16[1,2048,128]{2,1,0:T(8,128)(2,1)} %get-tuple-element.70), channel_id=1, source_target_pairs={{0,14},{1,15},{2,8},{3,9},{4,10},{5,11},{6,12},{7,13},{8,6},{9,7},... | collective-permute-start | bytes 1572872 | tf_op jit(solution)/shard_map/ppermute | solution.py:42
  80.7 25.6 %collective-permute-start.19 = (bf16[1,2048,128]{2,1,0:T(8,128)(2,1)}, bf16[1,2048,128]{2,1,0:T(8,128)(2,1)}, u32[]{:S(2)}, u32[]{:S(2)}) collective-permute-start(bf16[1,2048,128]{2,1,0:T(8,128)(2,1)} %get-tuple-element.71), channel_id=1, source_target_pairs={{0,4},{1,5},{2,6},{3,7},{4,0},{5,1},{6,2},{7,3},{8,12},{9,13},{10,... | collective-permute-start | bytes 1572872 | tf_op jit(solution)/shard_map/ppermute | solution.py:42
  92.7 12.5 %copy-start.4 = (bf16[1,2048,128]{2,1,0:T(8,128)(2,1)}, bf16[1,2048,128]{2,1,0:T(8,128)(2,1)S(1)}, u32[]{:S(2)}) copy-start(bf16[1,2048,128]{2,1,0:T(8,128)(2,1)S(1)} %collective-permute-done.17.refs_0_) | copy-start | bytes 1572868
  92.7 24.8 %collective-permute-start.14 = (bf16[1,2048,128]{2,1,0:T(8,128)(2,1)}, bf16[1,2048,128]{2,1,0:T(8,128)(2,1)}, u32[]{:S(2)}, u32[]{:S(2)}) collective-permute-start(bf16[1,2048,128]{2,1,0:T(8,128)(2,1)} %get-tuple-element.66), channel_id=1, source_target_pairs={{0,11},{1,10},{2,13},{3,12},{4,15},{5,14},{6,9},{7,8},{8,3},{9,2},... | collective-permute-start | bytes 1572872 | tf_op jit(solution)/shard_map/ppermute | solution.py:42
  96.5 31.8 %collective-permute-start.15 = (bf16[1,2048,128]{2,1,0:T(8,128)(2,1)}, bf16[1,2048,128]{2,1,0:T(8,128)(2,1)}, u32[]{:S(2)}, u32[]{:S(2)}) collective-permute-start(bf16[1,2048,128]{2,1,0:T(8,128)(2,1)} %get-tuple-element.67), channel_id=1, source_target_pairs={{0,15},{1,14},{2,9},{3,8},{4,11},{5,10},{6,13},{7,12},{8,7},{9,6},... | collective-permute-start | bytes 1572872 | tf_op jit(solution)/shard_map/ppermute | solution.py:42
  96.9 33.0 %collective-permute-start.16 = (bf16[1,2048,128]{2,1,0:T(8,128)(2,1)}, bf16[1,2048,128]{2,1,0:T(8,128)(2,1)}, u32[]{:S(2)}, u32[]{:S(2)}) collective-permute-start(bf16[1,2048,128]{2,1,0:T(8,128)(2,1)} %get-tuple-element.68), channel_id=1, source_target_pairs={{0,5},{1,4},{2,7},{3,6},{4,1},{5,0},{6,3},{7,2},{8,13},{9,12},{10,... | collective-permute-start | bytes 1572872 | tf_op jit(solution)/shard_map/ppermute | solution.py:42

commit v2 on v1

--- a/solution.py
+++ b/solution.py
@@ -200,7 +200,7 @@
     )(tcb, b, sq, mag)
 
 
-def finish_kernel(blocks, first, tcb, a, extras, *refs):
+def finish_kernel(blocks, first, near, tcb, a, extras, *refs):
     n = len(blocks)
     arrived, refs = refs[:n], refs[n if first else n + 1 :]
     out, raw, extra, done, block_to, column_from, raw_sems, extra_sems, done_sems = refs
@@ -211,12 +211,9 @@
         shard = shift_to(t, (dx, (4 - dy) % 4), flip)
         column = column_from[shard]
         here.append(column >= 0)
-        fetches.append(
-            (
-                pltpu.make_async_copy(extras.at[shard], extra.at[u], extra_sems.at[u]),
-                pltpu.make_async_copy(arrived[u].at[at], raw.at[u], raw_sems.at[u]),
-            )
-        )
+        fetches.append([pltpu.make_async_copy(extras.at[shard], extra.at[u], extra_sems.at[u])])
+        if not near:
+            fetches[u].append(pltpu.make_async_copy(arrived[u].at[at], raw.at[u], raw_sems.at[u]))
         target = out.at[:, columns(jnp.maximum(column, 0))]
         stores.append(pltpu.make_async_copy(done.at[u], target, done_sems.at[u]))
     for pair in fetches:
@@ -231,10 +228,11 @@
             parts = extra[u, 0:SCALE_ROWS, :].astype(F32)
             scale = parts[0:1] + parts[1:2] + parts[2:3]
             b = extra[u, SCALE_ROWS:EXTRA, :]
+            block = arrived[u].at[blocks[u][2]] if near else raw.at[u]
             for lo in range(0, a.shape[0], 256):
                 rows = slice(lo, lo + 256)
                 low_rank = jnp.dot(a[rows, :], b, preferred_element_type=F32)
-                combined = (raw[u, rows, :].astype(F32) + low_rank).astype(BF16).astype(F32)
+                combined = (block[rows, :].astype(F32) + low_rank).astype(BF16).astype(F32)
                 done[u, rows, :] = (combined * scale).astype(BF16)
             stores[u].start()
 
@@ -242,18 +240,18 @@
         pl.when(here[u])(stores[u].wait)
 
 
-def finish(tcb, a, extras, blocks, merged=None, width=None):
+def finish(tcb, a, extras, blocks, merged=None, width=None, near=False):
     rows, n, first = a.shape[0], len(blocks), merged is None
     arrays = [block[2] for block in blocks] + ([] if first else [merged])
     width = width if first else merged.shape[1]
     return pl.pallas_call(
-        functools.partial(finish_kernel, [(block[0], block[1], block[3]) for block in blocks], first),
+        functools.partial(finish_kernel, [(block[0], block[1], block[3]) for block in blocks], first, near),
         out_shape=jax.ShapeDtypeStruct((rows, width), BF16),
-        in_specs=[SMEM, VMEM, HBM] + [HBM] * len(arrays),
+        in_specs=[SMEM, VMEM, HBM] + [VMEM if near else HBM] * n + [HBM] * (len(arrays) - n),
         out_specs=HBM,
         input_output_aliases={} if first else {3 + n: 0},
         scratch_shapes=[
-            pltpu.VMEM((n, rows, BLK), BF16),
+            pltpu.VMEM((1 if near else n, rows, BLK), BF16),
             pltpu.VMEM((n, EXTRA, BLK), BF16),
             pltpu.VMEM((n, rows, BLK), BF16),
             pltpu.SMEM((16,), jnp.int32),
@@ -262,7 +260,7 @@
             pltpu.SemaphoreType.DMA((n,)),
             pltpu.SemaphoreType.DMA((n,)),
         ],
-        compiler_params=params(60),
+        compiler_params=params(12 if near else 60),
         cost_estimate=pl.CostEstimate(
             flops=2 * n * rows * BLK * 64, bytes_accessed=4 * n * rows * BLK, transcendentals=0
         ),
@@ -291,22 +289,25 @@
     for mask in B_MASKS[1:]:
         b = jnp.concatenate([b, send(b, fsdp_xor(mask))], axis=0)
     sq, a, b = squares(weight, a, b)
-    fourth, own, *single = pack(tcb, weight_then, [both(chips[3]), both(OWN)] + [(x,) for x in singles])
+    fourth, own = pack(tcb, weight_then, [both(chips[3]), both(OWN)])
     sq = sq + send(sq, fsdp_xor(1))
     sq, direct[:3], fourth = after((sq, direct[:3], fourth))
     direct[3] = send(fourth, tp_perm(chips[3]))
     for mask in (2, 6):
         sq = sq + send(sq, fsdp_xor(mask))
     extras = pack_extras(tcb, b, sq, magnitude[None, :])
+    extras, weight_then = after((extras, weight))
+    single = list(pack(tcb, weight_then, [(x,) for x in singles]))
     extras = lax.all_to_all(extras, "tp", split_axis=0, concat_axis=0, tiled=True)
     extras, direct[3], single, own = after((extras, direct[3], single, own))
     single = [send(m, tp_perm(*x)) for m, x in zip(single, singles)]
     blocks = [(OWN, 0, own, 0), (OWN, 1, send(own, tp_xor(1)), 1)]
     for o, m in zip(chips, direct):
         blocks += [(o, 0, m, 0), (o, 1, send(m, tp_xor(1)), 1)]
-    merged = finish(tcb, a, extras, blocks, width=weight.shape[1])
-    merged = finish(tcb, a, extras, [(*x, m, 0) for x, m in zip(singles[:3], single[:3])], merged)
-    return finish(tcb, a, extras, [(*x, m, 0) for x, m in zip(singles[3:], single[3:])], merged)
+    blocks += [(*x, m, 0) for x, m in zip(singles, single)]
+    merged = finish(tcb, a, extras, blocks[:10], width=weight.shape[1])
+    merged = finish(tcb, a, extras, blocks[10:13], merged)
+    return finish(tcb, a, extras, blocks[13:], merged, near=True)
 
 
 def solution(mesh):

time: 135 us -> 131 us (0.970)
  waiting for transfers between devices: 51.8 us -> 45.2 us
  local copies, waits for them, and re-layouts: 0.64 us -> 2.15 us
    all_to_all x1, waiting for transfers between devices: 10.2 us -> 5.82 us  [per_device(): lax.all_to_all(extras, 'tp', split_axis=0, concat_axis=0, tiled=True)]
    ppermute x25, waiting for transfers between devices: 41.6 us -> 39.4 us  [send(): return lax.ppermute(x, AXES, perm)]
    unnamed x18 -> x28, local copies, waits for them, and re-layouts: 0.04 us -> 1.56 us
    pallas_call x2 -> x3, Pallas kernels: 10.1 us -> 11.5 us  [pack(): pl.pallas_call(functools.partial(pack_kernel, messages), out_shape=[jax.S...]
  transfers between devices with their start and end apart: 26 -> 26, of which waited for: 12 -> 12; matrix products, arithmetic and copies ran while one was open for 2% -> 2% of each run, Pallas kernels for 21% -> 23%
where the time goes in v2:
time: 131 us; the launch traced here: 130 us
  starting transfers between devices  47.6 us (36%)
  waiting for transfers between devices  45.2 us (35%)
  Pallas kernels  32.8 us (25%)
  local copies, waits for them, and re-layouts  2.15 us (2%)
  other arithmetic  2.08 us (2%)
    ppermute x25, waiting for transfers between devices, send(): return lax.ppermute(x, AXES, perm)  39.4 us
    ppermute x25, starting transfers between devices, send(): return lax.ppermute(x, AXES, perm)  37.4 us
    pallas_call x3, Pallas kernels, finish(): pl.pallas_call(functools.partial(finish_kernel, [(block[0], block[1], blo...  12.7 us
    pallas_call x3, Pallas kernels, pack(): pl.pallas_call(functools.partial(pack_kernel, messages), out_shape=[jax.S...  11.5 us
    all_to_all x1, starting transfers between devices, per_device(): lax.all_to_all(extras, 'tp', split_axis=0, concat_axis=0, tiled=True)  10.2 us
    pallas_call x1, Pallas kernels, squares(): pl.pallas_call(squares_kernel, out_shape=[jax.ShapeDtypeStruct((1, width)...  6.54 us
    all_to_all x1, waiting for transfers between devices, per_device(): lax.all_to_all(extras, 'tp', split_axis=0, concat_axis=0, tiled=True)  5.82 us
  transfers between devices with their start and end apart: 26, of which 12 were waited for; matrix products, arithmetic and copies ran while one was open for 2% of the time, Pallas kernels for 23%

profile of v2, /device:TPU:27, one launch (start us, length us, event | category | flops | bytes accessed | tf_op | source)
XLA Modules:
  0.0 130.3 jit_solution(167991228868806503)
XLA Ops:
  0.0 0.5 collective-permute-start
  0.5 0.3 collective-permute-start.1
  0.7 3.9 %pack.3 = (bf16[2,2048,128]{2,1,0:T(8,128)(2,1)}, bf16[2,2048,128]{2,1,0:T(8,128)(2,1)}, bf16[2,2048,128]{2,1,0:T(8,128)(2,1)}) custom-call(s32[16,13]{1,0:T(8,128)} %tcb.13, bf16[2048,1664]{1,0:T(8,128)(2,1)} %w.3), custom_call_target="tpu_custom_call" | custom-call | bytes 6291456 | tf_op jit(solution)/shard_map/pack/pallas_call | solution.py:94
  4.7 0.9 collective-permute-start.2
  5.5 3.2 %collective-permute-done.2 = bf16[64,256]{1,0:T(8,128)(2,1)S(1)} collective-permute-done((bf16[64,256]{1,0:T(8,128)(2,1)S(1)}, bf16[64,256]{1,0:T(8,128)(2,1)S(1)}, u32[]{:S(2)}, u32[]{:S(2)}) %collective-permute-start.2) | collective-permute-done | bytes 32800 | tf_op jit(solution)/shard_map/ppermute | solution.py:42
  8.7 2.1 %collective-permute-start.3 = (bf16[64,512]{1,0:T(8,128)(2,1)S(1)}, bf16[64,512]{1,0:T(8,128)(2,1)S(1)}, u32[]{:S(2)}, u32[]{:S(2)}) collective-permute-start(bf16[64,512]{1,0:T(8,128)(2,1)S(1)} %pad_maximum_fusion.4), channel_id=1, source_target_pairs={{0,8},{1,9},{2,10},{3,11},{4,12},{5,13},{6,14},{7,15},{8,0},{9,1},... | collective-permute-start | bytes 196616 | tf_op jit(solution)/shard_map/ppermute | solution.py:42
  10.9 0.8 collective-permute-start.9
  11.6 0.7 collective-permute-start.10
  12.3 1.0 collective-permute-done.3
  13.3 2.2 %collective-permute-start.8 = (bf16[2,2048,128]{2,1,0:T(8,128)(2,1)}, bf16[2,2048,128]{2,1,0:T(8,128)(2,1)S(1)}, u32[]{:S(2)}, u32[]{:S(2)}) collective-permute-start(bf16[2,2048,128]{2,1,0:T(8,128)(2,1)} %get-tuple-element.53), channel_id=1, source_target_pairs={{0,8},{1,9},{2,10},{3,11},{4,12},{5,13},{6,14},{7,15},{8,0},{9,1},... | collective-permute-start | bytes 3145736 | tf_op jit(solution)/shard_map/ppermute | solution.py:42
  15.6 1.6 %collective-permute-start.5 = (bf16[16,1664]{1,0:T(8,128)(2,1)S(1)}, bf16[16,1664]{1,0:T(8,128)(2,1)S(1)}, u32[]{:S(2)}, u32[]{:S(2)}) collective-permute-start(bf16[16,1664]{1,0:T(8,128)(2,1)S(1)} %pad_maximum_fusion.5), channel_id=1, source_target_pairs={{0,32},{1,33},{2,34},{3,35},{4,36},{5,37},{6,38},{7,39},{8,40},{9,... | collective-permute-start | bytes 159752 | tf_op jit(solution)/shard_map/ppermute | solution.py:42
  17.2 1.8 %collective-permute-done.5 = bf16[16,1664]{1,0:T(8,128)(2,1)S(1)} collective-permute-done((bf16[16,1664]{1,0:T(8,128)(2,1)S(1)}, bf16[16,1664]{1,0:T(8,128)(2,1)S(1)}, u32[]{:S(2)}, u32[]{:S(2)}) %collective-permute-start.5) | collective-permute-done | bytes 53280 | tf_op jit(solution)/shard_map/ppermute | solution.py:42
  19.0 3.7 %collective-permute-start.6 = (bf16[32,1664]{1,0:T(8,128)(2,1)S(1)}, bf16[32,1664]{1,0:T(8,128)(2,1)S(1)}, u32[]{:S(2)}, u32[]{:S(2)}) collective-permute-start(bf16[32,1664]{1,0:T(8,128)(2,1)S(1)} %pad_maximum_fusion.3), channel_id=1, source_target_pairs={{0,96},{1,97},{2,98},{3,99},{4,100},{5,101},{6,102},{7,103},{8,104... | collective-permute-start | bytes 319496 | tf_op jit(solution)/shard_map/ppermute | solution.py:42
  22.7 4.9 %collective-permute-start.4 = (bf16[64,1024]{1,0:T(8,128)(2,1)S(1)}, bf16[64,1024]{1,0:T(8,128)(2,1)S(1)}, u32[]{:S(2)}, u32[]{:S(2)}) collective-permute-start(bf16[64,1024]{1,0:T(8,128)(2,1)S(1)} %pad_maximum_fusion.2), channel_id=1, source_target_pairs={{0,1},{1,0},{2,3},{3,2},{4,5},{5,4},{6,7},{7,6},{8,9},{9,8},{10,11... | collective-permute-start | bytes 393224 | tf_op jit(solution)/shard_map/ppermute | solution.py:42
  27.7 0.7 pad_maximum_fusion.1.b_rel
  28.4 0.3 collective-permute-done.4
  28.6 0.7 pad_maximum_fusion.a_rel
  29.4 6.5 %column_squares.1 = (f32[1,1664]{1,0:T(1,128)}, bf16[2048,64]{1,0:T(8,128)(2,1)}, bf16[64,1664]{1,0:T(8,128)(2,1)}) custom-call(bf16[2048,1664]{1,0:T(8,128)(2,1)} %w.3, bf16[64,2048]{1,0:T(8,128)(2,1)} %pad_maximum_fusion.a_rel, bf16[64,1664]{1,0:T(8,128)(2,1)} %pad_maximum_fusion.1.b_rel), custom_call_target="tpu_custom_call" | custom-call | flops 436207616 | bytes 6815744 | tf_op jit(solution)/shard_map/column_squares/pallas_call | solution.py:146
  35.9 1.6 %collective-permute-start.7 = (f32[1,1664]{1,0:T(1,128)}, f32[1,1664]{1,0:T(1,128)S(1)}, u32[]{:S(2)}, u32[]{:S(2)}) collective-permute-start(f32[1,1664]{1,0:T(1,128)} %get-tuple-element.52), channel_id=1, source_target_pairs={{0,16},{1,17},{2,18},{3,19},{4,20},{5,21},{6,22},{7,23},{8,24},{9,... | collective-permute-start | bytes 19976 | tf_op jit(solution)/shard_map/ppermute | solution.py:42
  37.5 3.6 %pack.4 = (bf16[2,2048,128]{2,1,0:T(8,128)(2,1)}, bf16[2,2048,128]{2,1,0:T(8,128)(2,1)}) custom-call(s32[16,13]{1,0:T(8,128)} %tcb.13, bf16[2048,1664]{1,0:T(8,128)(2,1)} %w.3), custom_call_target="tpu_custom_call" | custom-call | bytes 4194304 | tf_op jit(solution)/shard_map/pack/pallas_call | solution.py:94
  41.3 2.7 %collective-permute-start.21 = (bf16[2,2048,128]{2,1,0:T(8,128)(2,1)S(1)}, bf16[2,2048,128]{2,1,0:T(8,128)(2,1)}, u32[]{:S(2)}, u32[]{:S(2)}) collective-permute-start(bf16[2,2048,128]{2,1,0:T(8,128)(2,1)S(1)} %collective-permute-done.8.refs_2_), channel_id=1, source_target_pairs={{0,1},{1,0},{2,3},{3,2},{4,5},{5,4},{6,7},{7,6},{8,9},{9,8},{10,11... | collective-permute-start | bytes 3145736 | tf_op jit(solution)/shard_map/ppermute | solution.py:42
  44.1 0.6 collective-permute-start.11
  44.7 1.9 %collective-permute-done.11 = f32[1,1664]{1,0:T(1,128)S(1)} collective-permute-done((f32[1,1664]{1,0:T(1,128)S(1)}, f32[1,1664]{1,0:T(1,128)S(1)}, u32[]{:S(2)}, u32[]{:S(2)}) %collective-permute-start.11) | collective-permute-done | bytes 6688 | tf_op jit(solution)/shard_map/ppermute | solution.py:42
  46.6 3.0 %collective-permute-start.12 = (f32[1,1664]{1,0:T(1,128)S(1)}, f32[1,1664]{1,0:T(1,128)S(1)}, u32[]{:S(2)}, u32[]{:S(2)}) collective-permute-start(f32[1,1664]{1,0:T(1,128)S(1)} %add.10), channel_id=1, source_target_pairs={{0,96},{1,97},{2,98},{3,99},{4,100},{5,101},{6,102},{7,103},{8,104... | collective-permute-start | bytes 19976 | tf_op jit(solution)/shard_map/ppermute | solution.py:42
  49.6 0.6 broadcast_in_dim.3.mag
  50.2 0.4 collective-permute-done.12
  50.6 0.6 add.11.sq
  51.2 2.1 %pack_extras.1 = bf16[16,80,128]{2,1,0:T(8,128)(2,1)} custom-call(s32[16,13]{1,0:T(8,128)} %tcb.13, bf16[64,1664]{1,0:T(8,128)(2,1)} %get-tuple-element.51.b, f32[1,1664]{1,0:T(1,128)} %add.11.sq, f32[1,1664]{1,0:T(1,128)} %broadcast_in_dim.3.mag), custom_call_target="tpu_custom_call" | custom-call | tf_op jit(solution)/shard_map/pack_extras/pallas_call | solution.py:187
  53.3 10.2 %all-to-all-start = ((bf16[16,80,128]{2,1,0:T(8,128)(2,1)}), bf16[16,80,128]{2,1,0:T(8,128)(2,1)S(1)}, u32[]{:S(2)}, u32[]{:S(2)}) async-start(bf16[16,80,128]{2,1,0:T(8,128)(2,1)} %pack_extras.1), calls=%async_computation | async-start | bytes 655360 | tf_op jit(solution)/shard_map/all_to_all | solution.py:301
  63.5 0.4 collective-permute-start.22
  64.0 4.0 %pack.5 = (bf16[1,2048,128]{2,1,0:T(8,128)(2,1)}, bf16[1,2048,128]{2,1,0:T(8,128)(2,1)}, bf16[1,2048,128]{2,1,0:T(8,128)(2,1)}, bf16[1,2048,128]{2,1,0:T(8,128)(...) custom-call(s32[16,13]{1,0:T(8,128)} %tcb.13, bf16[2048,1664]{1,0:T(8,128)(2,1)} %w.3), custom_call_target="tpu_custom_call" | custom-call | bytes 6291456 | tf_op jit(solution)/shard_map/pack/pallas_call | solution.py:94
  68.1 5.8 %all-to-all-done.extras = bf16[16,80,128]{2,1,0:T(8,128)(2,1)S(1)} async-done(((bf16[16,80,128]{2,1,0:T(8,128)(2,1)}), bf16[16,80,128]{2,1,0:T(8,128)(2,1)S(1)}, u32[]{:S(2)}, u32[]{:S(2)}) %all-to-all-start) | async-done | bytes 327712 | tf_op jit(solution)/shard_map/all_to_all | solution.py:301
  73.9 0.4 collective-permute-start.20
  74.4 0.7 collective-permute-start.17
  75.1 3.2 %collective-permute-start.18 = (bf16[1,2048,128]{2,1,0:T(8,128)(2,1)}, bf16[1,2048,128]{2,1,0:T(8,128)(2,1)}, u32[]{:S(2)}, u32[]{:S(2)}) collective-permute-start(bf16[1,2048,128]{2,1,0:T(8,128)(2,1)} %get-tuple-element.74), channel_id=1, source_target_pairs={{0,14},{1,15},{2,8},{3,9},{4,10},{5,11},{6,12},{7,13},{8,6},{9,7},... | collective-permute-start | bytes 1572872 | tf_op jit(solution)/shard_map/ppermute | solution.py:42
  78.3 0.6 collective-permute-start.19
  78.9 11.4 %collective-permute-done.17.refs_0_ = bf16[1,2048,128]{2,1,0:T(8,128)(2,1)S(1)} collective-permute-done((bf16[1,2048,128]{2,1,0:T(8,128)(2,1)}, bf16[1,2048,128]{2,1,0:T(8,128)(2,1)S(1)}, u32[]{:S(2)}, u32[]{:S(2)}) %collective-permute-start.17) | collective-permute-done | bytes 524320 | tf_op jit(solution)/shard_map/ppermute | solution.py:42
  90.3 3.8 %collective-permute-start.14 = (bf16[1,2048,128]{2,1,0:T(8,128)(2,1)}, bf16[1,2048,128]{2,1,0:T(8,128)(2,1)S(1)}, u32[]{:S(2)}, u32[]{:S(2)}) collective-permute-start(bf16[1,2048,128]{2,1,0:T(8,128)(2,1)} %get-tuple-element.70), channel_id=1, source_target_pairs={{0,11},{1,10},{2,13},{3,12},{4,15},{5,14},{6,9},{7,8},{8,3},{9,2},... | collective-permute-start | bytes 1572872 | tf_op jit(solution)/shard_map/ppermute | solution.py:42
  94.1 0.5 collective-permute-start.15
  94.5 0.5 copy-done.7
  95.0 1.0 copy-done.8
  96.0 2.0 %collective-permute-start.16 = (bf16[1,2048,128]{2,1,0:T(8,128)(2,1)}, bf16[1,2048,128]{2,1,0:T(8,128)(2,1)S(1)}, u32[]{:S(2)}, u32[]{:S(2)}) collective-permute-start(bf16[1,2048,128]{2,1,0:T(8,128)(2,1)} %get-tuple-element.72), channel_id=1, source_target_pairs={{0,5},{1,4},{2,7},{3,6},{4,1},{5,0},{6,3},{7,2},{8,13},{9,12},{10,... | collective-permute-start | bytes 1572872 | tf_op jit(solution)/shard_map/ppermute | solution.py:42
  98.0 5.7 %finish.3.refs_3_ = bf16[2048,1664]{1,0:T(8,128)(2,1)} custom-call(s32[16,13]{1,0:T(8,128)} %tcb.13, bf16[2048,64]{1,0:T(8,128)(2,1)} %get-tuple-element.50.a, bf16[16,80,128]{2,1,0:T(8,128)(2,1)} %copy-done, bf16[2,2048,128]{2,1,0:T(8,128)(2,1)} %get-tuple-element.76.refs_0_, bf16[2,2048,128]{2,1,0:T(8,128)(2,1)} %copy-done.7, ...), custom_call_target="tpu_custom_call" | custom-call | flops 335544320 | bytes 10485760 | tf_op jit(solution)/shard_map/finish/pallas_call | solution.py:247
  103.9 4.2 %finish.4.refs_3_ = bf16[2048,1664]{1,0:T(8,128)(2,1)} custom-call(s32[16,13]{1,0:T(8,128)} %tcb.13, bf16[2048,64]{1,0:T(8,128)(2,1)} %get-tuple-element.50.a, bf16[16,80,128]{2,1,0:T(8,128)(2,1)} %copy-done, bf16[1,2048,128]{2,1,0:T(8,128)(2,1)} %copy-done.9, bf16[1,2048,128]{2,1,0:T(8,128)(2,1)} %collective-permute-done.18.refs_1_, ...), custom_call_target="tpu_custom_call", output_to_operand_aliasing={{}: (6, {})} | custom-call | flops 100663296 | bytes 3145728 | tf_op jit(solution)/shard_map/finish/pallas_call | solution.py:247
  108.0 6.9 %collective-permute-done.14.refs_0_ = bf16[1,2048,128]{2,1,0:T(8,128)(2,1)S(1)} collective-permute-done((bf16[1,2048,128]{2,1,0:T(8,128)(2,1)}, bf16[1,2048,128]{2,1,0:T(8,128)(2,1)S(1)}, u32[]{:S(2)}, u32[]{:S(2)}) %collective-permute-start.14) | collective-permute-done | bytes 524320 | tf_op jit(solution)/shard_map/ppermute | solution.py:42
  114.9 10.9 %collective-permute-done.15.refs_1_ = bf16[1,2048,128]{2,1,0:T(8,128)(2,1)S(1)} collective-permute-done((bf16[1,2048,128]{2,1,0:T(8,128)(2,1)}, bf16[1,2048,128]{2,1,0:T(8,128)(2,1)S(1)}, u32[]{:S(2)}, u32[]{:S(2)}) %collective-permute-start.15) | collective-permute-done | bytes 524320 | tf_op jit(solution)/shard_map/ppermute | solution.py:42
  125.8 1.6 %collective-permute-done.16.refs_2_ = bf16[1,2048,128]{2,1,0:T(8,128)(2,1)S(1)} collective-permute-done((bf16[1,2048,128]{2,1,0:T(8,128)(2,1)}, bf16[1,2048,128]{2,1,0:T(8,128)(2,1)S(1)}, u32[]{:S(2)}, u32[]{:S(2)}) %collective-permute-start.16) | collective-permute-done | bytes 524320 | tf_op jit(solution)/shard_map/ppermute | solution.py:42
  127.4 2.8 %finish.5 = bf16[2048,1664]{1,0:T(8,128)(2,1)} custom-call(s32[16,13]{1,0:T(8,128)S(1)} %copy-done.3, bf16[2048,64]{1,0:T(8,128)(2,1)S(1)} %copy-done.2, bf16[16,80,128]{2,1,0:T(8,128)(2,1)S(1)} %copy-done.1, bf16[1,2048,128]{2,1,0:T(8,128)(2,1)S(1)} %collective-permute-done.14.refs_0_, ...), custom_call_target="tpu_custom_call", output_to_operand_aliasing={{}: (6, {})} | custom-call | flops 100663296 | bytes 3145728 | tf_op jit(solution)/shard_map/finish/pallas_call | solution.py:247
  (51 shorter events, 0.6 us)
Async XLA Ops:
  0.0 4.6 %copy-start.11 = (bf16[128,64]{0,1:T(8,128)(2,1)S(1)}, bf16[128,64]{0,1:T(8,128)(2,1)}, u32[]{:S(2)}) copy-start(bf16[128,64]{0,1:T(8,128)(2,1)} %param.6) | copy-start | bytes 49156
  0.0 4.6 %copy-start.10 = (bf16[8,1664]{1,0:T(8,128)(2,1)S(1)}, bf16[8,1664]{1,0:T(8,128)(2,1)}, u32[]{:S(2)}) copy-start(bf16[8,1664]{1,0:T(8,128)(2,1)} %param.7) | copy-start | bytes 79876
  0.0 4.6 %collective-permute-start = (bf16[64,128]{1,0:T(8,128)(2,1)}, bf16[64,128]{1,0:T(8,128)(2,1)S(1)}, u32[]{:S(2)}, u32[]{:S(2)}) collective-permute-start(bf16[64,128]{1,0:T(8,128)(2,1)} %bitcast.1), channel_id=1, source_target_pairs={{0,2},{1,3},{2,0},{3,1},{4,6},{5,7},{6,4},{7,5},{8,10},{9,11},{10,... | collective-permute-start | bytes 49160 | tf_op jit(solution)/shard_map/ppermute | solution.py:42
  0.5 4.2 %collective-permute-start.1 = (bf16[8,1664]{1,0:T(8,128)(2,1)}, bf16[8,1664]{1,0:T(8,128)(2,1)S(1)}, u32[]{:S(2)}, u32[]{:S(2)}) collective-permute-start(bf16[8,1664]{1,0:T(8,128)(2,1)} %param.7), channel_id=1, source_target_pairs={{0,16},{1,17},{2,18},{3,19},{4,20},{5,21},{6,22},{7,23},{8,24},{9,... | collective-permute-start | bytes 79880 | tf_op jit(solution)/shard_map/ppermute | solution.py:42
  4.7 4.1 %collective-permute-start.2 = (bf16[64,256]{1,0:T(8,128)(2,1)S(1)}, bf16[64,256]{1,0:T(8,128)(2,1)S(1)}, u32[]{:S(2)}, u32[]{:S(2)}) collective-permute-start(bf16[64,256]{1,0:T(8,128)(2,1)S(1)} %pad_maximum_fusion.6), channel_id=1, source_target_pairs={{0,6},{1,7},{2,4},{3,5},{4,2},{5,3},{6,0},{7,1},{8,14},{9,15},{10,... | collective-permute-start | bytes 98312 | tf_op jit(solution)/shard_map/ppermute | solution.py:42
  8.7 4.6 %collective-permute-start.3 = (bf16[64,512]{1,0:T(8,128)(2,1)S(1)}, bf16[64,512]{1,0:T(8,128)(2,1)S(1)}, u32[]{:S(2)}, u32[]{:S(2)}) collective-permute-start(bf16[64,512]{1,0:T(8,128)(2,1)S(1)} %pad_maximum_fusion.4), channel_id=1, source_target_pairs={{0,8},{1,9},{2,10},{3,11},{4,12},{5,13},{6,14},{7,15},{8,0},{9,1},... | collective-permute-start | bytes 196616 | tf_op jit(solution)/shard_map/ppermute | solution.py:42
  10.9 30.3 %collective-permute-start.9 = (bf16[2,2048,128]{2,1,0:T(8,128)(2,1)}, bf16[2,2048,128]{2,1,0:T(8,128)(2,1)S(1)}, u32[]{:S(2)}, u32[]{:S(2)}) collective-permute-start(bf16[2,2048,128]{2,1,0:T(8,128)(2,1)} %get-tuple-element.54), channel_id=1, source_target_pairs={{0,2},{1,3},{2,4},{3,5},{4,6},{5,7},{6,0},{7,1},{8,10},{9,11},{10,... | collective-permute-start | bytes 3145736 | tf_op jit(solution)/shard_map/ppermute | solution.py:42
  11.6 29.6 %collective-permute-start.10 = (bf16[2,2048,128]{2,1,0:T(8,128)(2,1)}, bf16[2,2048,128]{2,1,0:T(8,128)(2,1)S(1)}, u32[]{:S(2)}, u32[]{:S(2)}) collective-permute-start(bf16[2,2048,128]{2,1,0:T(8,128)(2,1)} %get-tuple-element.55), channel_id=1, source_target_pairs={{0,6},{1,7},{2,0},{3,1},{4,2},{5,3},{6,4},{7,5},{8,14},{9,15},{10,... | collective-permute-start | bytes 3145736 | tf_op jit(solution)/shard_map/ppermute | solution.py:42
  13.3 27.9 %collective-permute-start.8 = (bf16[2,2048,128]{2,1,0:T(8,128)(2,1)}, bf16[2,2048,128]{2,1,0:T(8,128)(2,1)S(1)}, u32[]{:S(2)}, u32[]{:S(2)}) collective-permute-start(bf16[2,2048,128]{2,1,0:T(8,128)(2,1)} %get-tuple-element.53), channel_id=1, source_target_pairs={{0,8},{1,9},{2,10},{3,11},{4,12},{5,13},{6,14},{7,15},{8,0},{9,1},... | collective-permute-start | bytes 3145736 | tf_op jit(solution)/shard_map/ppermute | solution.py:42
  15.6 3.5 %collective-permute-start.5 = (bf16[16,1664]{1,0:T(8,128)(2,1)S(1)}, bf16[16,1664]{1,0:T(8,128)(2,1)S(1)}, u32[]{:S(2)}, u32[]{:S(2)}) collective-permute-start(bf16[16,1664]{1,0:T(8,128)(2,1)S(1)} %pad_maximum_fusion.5), channel_id=1, source_target_pairs={{0,32},{1,33},{2,34},{3,35},{4,36},{5,37},{6,38},{7,39},{8,40},{9,... | collective-permute-start | bytes 159752 | tf_op jit(solution)/shard_map/ppermute | solution.py:42
  19.0 8.6 %collective-permute-start.6 = (bf16[32,1664]{1,0:T(8,128)(2,1)S(1)}, bf16[32,1664]{1,0:T(8,128)(2,1)S(1)}, u32[]{:S(2)}, u32[]{:S(2)}) collective-permute-start(bf16[32,1664]{1,0:T(8,128)(2,1)S(1)} %pad_maximum_fusion.3), channel_id=1, source_target_pairs={{0,96},{1,97},{2,98},{3,99},{4,100},{5,101},{6,102},{7,103},{8,104... | collective-permute-start | bytes 319496 | tf_op jit(solution)/shard_map/ppermute | solution.py:42
  22.7 5.9 %collective-permute-start.4 = (bf16[64,1024]{1,0:T(8,128)(2,1)S(1)}, bf16[64,1024]{1,0:T(8,128)(2,1)S(1)}, u32[]{:S(2)}, u32[]{:S(2)}) collective-permute-start(bf16[64,1024]{1,0:T(8,128)(2,1)S(1)} %pad_maximum_fusion.2), channel_id=1, source_target_pairs={{0,1},{1,0},{2,3},{3,2},{4,5},{5,4},{6,7},{7,6},{8,9},{9,8},{10,11... | collective-permute-start | bytes 393224 | tf_op jit(solution)/shard_map/ppermute | solution.py:42
  29.4 20.2 %copy-start.12 = (f32[1664]{0:T(1024)S(1)}, f32[1664]{0:T(1024)}, u32[]{:S(2)}) copy-start(f32[1664]{0:T(1024)} %param.8) | copy-start | bytes 19972
  35.9 5.2 %copy-start.13 = (f32[1,1664]{1,0:T(1,128)S(1)}, f32[1,1664]{1,0:T(1,128)}, u32[]{:S(2)}) copy-start(f32[1,1664]{1,0:T(1,128)} %get-tuple-element.52) | copy-start | bytes 19972
  35.9 5.2 %collective-permute-start.7 = (f32[1,1664]{1,0:T(1,128)}, f32[1,1664]{1,0:T(1,128)S(1)}, u32[]{:S(2)}, u32[]{:S(2)}) collective-permute-start(f32[1,1664]{1,0:T(1,128)} %get-tuple-element.52), channel_id=1, source_target_pairs={{0,16},{1,17},{2,18},{3,19},{4,20},{5,21},{6,22},{7,23},{8,24},{9,... | collective-permute-start | bytes 19976 | tf_op jit(solution)/shard_map/ppermute | solution.py:42
  41.2 56.8 %copy-start.4 = (bf16[2,2048,128]{2,1,0:T(8,128)(2,1)}, bf16[2,2048,128]{2,1,0:T(8,128)(2,1)S(1)}, u32[]{:S(2)}) copy-start(bf16[2,2048,128]{2,1,0:T(8,128)(2,1)S(1)} %collective-permute-done.9.refs_4_) | copy-start | bytes 3145732
  41.2 56.8 %copy-start.5 = (bf16[2,2048,128]{2,1,0:T(8,128)(2,1)}, bf16[2,2048,128]{2,1,0:T(8,128)(2,1)S(1)}, u32[]{:S(2)}) copy-start(bf16[2,2048,128]{2,1,0:T(8,128)(2,1)S(1)} %collective-permute-done.10.refs_6_) | copy-start | bytes 3145732
  41.2 52.8 %copy-start.6 = (bf16[2,2048,128]{2,1,0:T(8,128)(2,1)}, bf16[2,2048,128]{2,1,0:T(8,128)(2,1)S(1)}, u32[]{:S(2)}) copy-start(bf16[2,2048,128]{2,1,0:T(8,128)(2,1)S(1)} %collective-permute-done.8.refs_2_) | copy-start | bytes 3145732
  41.2 32.7 %collective-permute-start.13 = (bf16[2,2048,128]{2,1,0:T(8,128)(2,1)}, bf16[2,2048,128]{2,1,0:T(8,128)(2,1)}, u32[]{:S(2)}, u32[]{:S(2)}) collective-permute-start(bf16[2,2048,128]{2,1,0:T(8,128)(2,1)} %get-tuple-element.60), channel_id=1, source_target_pairs={{0,12},{1,13},{2,14},{3,15},{4,8},{5,9},{6,10},{7,11},{8,4},{9,5},... | collective-permute-start | bytes 3145736 | tf_op jit(solution)/shard_map/ppermute | solution.py:42
  41.3 33.1 %collective-permute-start.21 = (bf16[2,2048,128]{2,1,0:T(8,128)(2,1)S(1)}, bf16[2,2048,128]{2,1,0:T(8,128)(2,1)}, u32[]{:S(2)}, u32[]{:S(2)}) collective-permute-start(bf16[2,2048,128]{2,1,0:T(8,128)(2,1)S(1)} %collective-permute-done.8.refs_2_), channel_id=1, source_target_pairs={{0,1},{1,0},{2,3},{3,2},{4,5},{5,4},{6,7},{7,6},{8,9},{9,8},{10,11... | collective-permute-start | bytes 3145736 | tf_op jit(solution)/shard_map/ppermute | solution.py:42
  44.1 2.5 %collective-permute-start.11 = (f32[1,1664]{1,0:T(1,128)S(1)}, f32[1,1664]{1,0:T(1,128)S(1)}, u32[]{:S(2)}, u32[]{:S(2)}) collective-permute-start(f32[1,1664]{1,0:T(1,128)S(1)} %add.9), channel_id=1, source_target_pairs={{0,32},{1,33},{2,34},{3,35},{4,36},{5,37},{6,38},{7,39},{8,40},{9,... | collective-permute-start | bytes 19976 | tf_op jit(solution)/shard_map/ppermute | solution.py:42
  46.6 4.1 %collective-permute-start.12 = (f32[1,1664]{1,0:T(1,128)S(1)}, f32[1,1664]{1,0:T(1,128)S(1)}, u32[]{:S(2)}, u32[]{:S(2)}) collective-permute-start(f32[1,1664]{1,0:T(1,128)S(1)} %add.10), channel_id=1, source_target_pairs={{0,96},{1,97},{2,98},{3,99},{4,100},{5,101},{6,102},{7,103},{8,104... | collective-permute-start | bytes 19976 | tf_op jit(solution)/shard_map/ppermute | solution.py:42
  53.3 20.6 %all-to-all-start = ((bf16[16,80,128]{2,1,0:T(8,128)(2,1)}), bf16[16,80,128]{2,1,0:T(8,128)(2,1)S(1)}, u32[]{:S(2)}, u32[]{:S(2)}) async-start(bf16[16,80,128]{2,1,0:T(8,128)(2,1)} %pack_extras.1), calls=%async_computation | async-start | bytes 655360 | tf_op jit(solution)/shard_map/all_to_all | solution.py:301
  63.5 11.6 %collective-permute-start.22 = (bf16[2,2048,128]{2,1,0:T(8,128)(2,1)S(1)}, bf16[2,2048,128]{2,1,0:T(8,128)(2,1)}, u32[]{:S(2)}, u32[]{:S(2)}) collective-permute-start(bf16[2,2048,128]{2,1,0:T(8,128)(2,1)S(1)} %collective-permute-done.9.refs_4_), channel_id=1, source_target_pairs={{0,1},{1,0},{2,3},{3,2},{4,5},{5,4},{6,7},{7,6},{8,9},{9,8},{10,11... | collective-permute-start | bytes 3145736 | tf_op jit(solution)/shard_map/ppermute | solution.py:42
  63.9 14.4 %collective-permute-start.23 = (bf16[2,2048,128]{2,1,0:T(8,128)(2,1)S(1)}, bf16[2,2048,128]{2,1,0:T(8,128)(2,1)}, u32[]{:S(2)}, u32[]{:S(2)}) collective-permute-start(bf16[2,2048,128]{2,1,0:T(8,128)(2,1)S(1)} %collective-permute-done.10.refs_6_), channel_id=1, source_target_pairs={{0,1},{1,0},{2,3},{3,2},{4,5},{5,4},{6,7},{7,6},{8,9},{9,8},{10,11... | collective-permute-start | bytes 3145736 | tf_op jit(solution)/shard_map/ppermute | solution.py:42
  73.9 24.1 %copy-start = (bf16[16,80,128]{2,1,0:T(8,128)(2,1)}, bf16[16,80,128]{2,1,0:T(8,128)(2,1)S(1)}, u32[]{:S(2)}) copy-start(bf16[16,80,128]{2,1,0:T(8,128)(2,1)S(1)} %all-to-all-done.extras) | copy-start | bytes 983044
  73.9 20.1 %collective-permute-start.20 = (bf16[2,2048,128]{2,1,0:T(8,128)(2,1)}, bf16[2,2048,128]{2,1,0:T(8,128)(2,1)S(1)}, u32[]{:S(2)}, u32[]{:S(2)}) collective-permute-start(bf16[2,2048,128]{2,1,0:T(8,128)(2,1)} %get-tuple-element.76.refs_0_), channel_id=1, source_target_pairs={{0,1},{1,0},{2,3},{3,2},{4,5},{5,4},{6,7},{7,6},{8,9},{9,8},{10,11... | collective-permute-start | bytes 3145736 | tf_op jit(solution)/shard_map/ppermute | solution.py:42
  74.3 20.8 %collective-permute-start.24 = (bf16[2,2048,128]{2,1,0:T(8,128)(2,1)}, bf16[2,2048,128]{2,1,0:T(8,128)(2,1)S(1)}, u32[]{:S(2)}, u32[]{:S(2)}) collective-permute-start(bf16[2,2048,128]{2,1,0:T(8,128)(2,1)} %collective-permute-done.13.refs_8_), channel_id=1, source_target_pairs={{0,1},{1,0},{2,3},{3,2},{4,5},{5,4},{6,7},{7,6},{8,9},{9,8},{10,11... | collective-permute-start | bytes 3145736 | tf_op jit(solution)/shard_map/ppermute | solution.py:42
  74.4 15.9 %collective-permute-start.17 = (bf16[1,2048,128]{2,1,0:T(8,128)(2,1)}, bf16[1,2048,128]{2,1,0:T(8,128)(2,1)S(1)}, u32[]{:S(2)}, u32[]{:S(2)}) collective-permute-start(bf16[1,2048,128]{2,1,0:T(8,128)(2,1)} %get-tuple-element.73), channel_id=1, source_target_pairs={{0,10},{1,11},{2,12},{3,13},{4,14},{5,15},{6,8},{7,9},{8,2},{9,3},... | collective-permute-start | bytes 1572872 | tf_op jit(solution)/shard_map/ppermute | solution.py:42
  75.1 28.6 %collective-permute-start.18 = (bf16[1,2048,128]{2,1,0:T(8,128)(2,1)}, bf16[1,2048,128]{2,1,0:T(8,128)(2,1)}, u32[]{:S(2)}, u32[]{:S(2)}) collective-permute-start(bf16[1,2048,128]{2,1,0:T(8,128)(2,1)} %get-tuple-element.74), channel_id=1, source_target_pairs={{0,14},{1,15},{2,8},{3,9},{4,10},{5,11},{6,12},{7,13},{8,6},{9,7},... | collective-permute-start | bytes 1572872 | tf_op jit(solution)/shard_map/ppermute | solution.py:42
  78.3 25.6 %collective-permute-start.19 = (bf16[1,2048,128]{2,1,0:T(8,128)(2,1)}, bf16[1,2048,128]{2,1,0:T(8,128)(2,1)}, u32[]{:S(2)}, u32[]{:S(2)}) collective-permute-start(bf16[1,2048,128]{2,1,0:T(8,128)(2,1)} %get-tuple-element.75), channel_id=1, source_target_pairs={{0,4},{1,5},{2,6},{3,7},{4,0},{5,1},{6,2},{7,3},{8,12},{9,13},{10,... | collective-permute-start | bytes 1572872 | tf_op jit(solution)/shard_map/ppermute | solution.py:42
  90.3 7.7 %copy-start.9 = (bf16[1,2048,128]{2,1,0:T(8,128)(2,1)}, bf16[1,2048,128]{2,1,0:T(8,128)(2,1)S(1)}, u32[]{:S(2)}) copy-start(bf16[1,2048,128]{2,1,0:T(8,128)(2,1)S(1)} %collective-permute-done.17.refs_0_) | copy-start | bytes 1572868
  90.3 24.6 %collective-permute-start.14 = (bf16[1,2048,128]{2,1,0:T(8,128)(2,1)}, bf16[1,2048,128]{2,1,0:T(8,128)(2,1)S(1)}, u32[]{:S(2)}, u32[]{:S(2)}) collective-permute-start(bf16[1,2048,128]{2,1,0:T(8,128)(2,1)} %get-tuple-element.70), channel_id=1, source_target_pairs={{0,11},{1,10},{2,13},{3,12},{4,15},{5,14},{6,9},{7,8},{8,3},{9,2},... | collective-permute-start | bytes 1572872 | tf_op jit(solution)/shard_map/ppermute | solution.py:42
  94.1 1.0 copy-start.7
  94.1 31.8 %collective-permute-start.15 = (bf16[1,2048,128]{2,1,0:T(8,128)(2,1)}, bf16[1,2048,128]{2,1,0:T(8,128)(2,1)S(1)}, u32[]{:S(2)}, u32[]{:S(2)}) collective-permute-start(bf16[1,2048,128]{2,1,0:T(8,128)(2,1)} %get-tuple-element.71), channel_id=1, source_target_pairs={{0,15},{1,14},{2,9},{3,8},{4,11},{5,10},{6,13},{7,12},{8,7},{9,6},... | collective-permute-start | bytes 1572872 | tf_op jit(solution)/shard_map/ppermute | solution.py:42
  95.0 1.0 copy-start.8
  96.0 31.4 %collective-permute-start.16 = (bf16[1,2048,128]{2,1,0:T(8,128)(2,1)}, bf16[1,2048,128]{2,1,0:T(8,128)(2,1)S(1)}, u32[]{:S(2)}, u32[]{:S(2)}) collective-permute-start(bf16[1,2048,128]{2,1,0:T(8,128)(2,1)} %get-tuple-element.72), channel_id=1, source_target_pairs={{0,5},{1,4},{2,7},{3,6},{4,1},{5,0},{6,3},{7,2},{8,13},{9,12},{10,... | collective-permute-start | bytes 1572872 | tf_op jit(solution)/shard_map/ppermute | solution.py:42
  103.7 23.7 %copy-start.1 = (bf16[16,80,128]{2,1,0:T(8,128)(2,1)S(1)}, bf16[16,80,128]{2,1,0:T(8,128)(2,1)}, u32[]{:S(2)}) copy-start(bf16[16,80,128]{2,1,0:T(8,128)(2,1)} %copy-done) | copy-start | bytes 983044
  103.7 23.7 %copy-start.2 = (bf16[2048,64]{1,0:T(8,128)(2,1)S(1)}, bf16[2048,64]{1,0:T(8,128)(2,1)}, u32[]{:S(2)}) copy-start(bf16[2048,64]{1,0:T(8,128)(2,1)} %get-tuple-element.50.a) | copy-start | bytes 786436
  103.7 23.6 %copy-start.3 = (s32[16,13]{1,0:T(8,128)S(1)}, s32[16,13]{1,0:T(8,128)}, u32[]{:S(2)}) copy-start(s32[16,13]{1,0:T(8,128)} %tcb.13) | copy-start | bytes 2500

commit v3 on v2

--- a/solution.py
+++ b/solution.py
@@ -12,7 +12,7 @@
 SCALE_ROWS = 16
 EXTRA = 80
 OWN = (0, 0)
-A_MASKS = (2, 6, 8, 1)
+A_MASKS = (8, 2, 6, 1)
 B_MASKS = (1, 2, 6)
 BF16, F32 = jnp.bfloat16, jnp.float32
 HBM = pl.BlockSpec(memory_space=pltpu.HBM)
@@ -126,7 +126,7 @@
     for i in range(16):
         rel = i ^ t
         r0, r1, r2, r3 = rel & 1, (rel >> 1) & 1, (rel >> 2) & 1, (rel >> 3) & 1
-        slot = (r1 ^ r2) | (r2 << 1) | (r3 << 2) | (r0 << 3)
+        slot = r3 | ((r1 ^ r2) << 1) | (r2 << 2) | (r0 << 3)
         a_ord[i * 128 : (i + 1) * 128, :] = a_rel[:, columns(slot)].astype(F32).T.astype(BF16)
     sums = [jnp.zeros((8, min(256, width - lo)), F32) for lo in range(0, width, 256)]
     for i in range(count):
@@ -274,20 +274,21 @@
     chips = ((1, 0), (0, 1), (0, 3), (1, 2))
     singles = [(o, flip) for flip in range(2) for o in ((1, 1), (1, 3), (0, 2))]
     head = list(pack(tcb, weight, [both(o) for o in chips[:3]]))
-    a, b = adapter_down_factor.T, adapter_up_factor
-    a = jnp.concatenate([a, send(a, tp_xor(A_MASKS[0]))], axis=1)
-    b = jnp.concatenate([b, send(b, fsdp_xor(B_MASKS[0]))], axis=0)
+    direct = [None] * 4
+
+    def gather(a, b, i):
+        a = jnp.concatenate([a, send(a, tp_xor(A_MASKS[i]))], axis=1)
+        return a, jnp.concatenate([b, send(b, fsdp_xor(B_MASKS[i]))], axis=0)
+
+    a, b = gather(adapter_down_factor.T, adapter_up_factor, 0)
     a, b, head = after((a, b, head))
-    direct = [None] * 4
+    direct[0] = send(head[0], tp_perm(chips[0]))
+    a, b = after(gather(a, b, 1))
+    a, b = gather(a, b, 2)
+    a, head[1:3], weight_then = after((a, head[1:3], weight))
     for n in (1, 2):
         direct[n] = send(head[n], tp_perm(chips[n]))
-    for mask in A_MASKS[1:3]:
-        a = jnp.concatenate([a, send(a, tp_xor(mask))], axis=1)
-    a, head[0], weight_then = after((a, head[0], weight))
-    direct[0] = send(head[0], tp_perm(chips[0]))
     a = jnp.concatenate([a, send(a, tp_xor(A_MASKS[3]))], axis=1)
-    for mask in B_MASKS[1:]:
-        b = jnp.concatenate([b, send(b, fsdp_xor(mask))], axis=0)
     sq, a, b = squares(weight, a, b)
     fourth, own = pack(tcb, weight_then, [both(chips[3]), both(OWN)])
     sq = sq + send(sq, fsdp_xor(1))

time: 131 us -> 128 us (0.977)
  starting transfers between devices: 47.6 us -> 45.9 us
    all_to_all x1, waiting for transfers between devices: 5.82 us -> 4.29 us  [per_device(): lax.all_to_all(extras, 'tp', split_axis=0, concat_axis=0, tiled=True)]
  transfers between devices with their start and end apart: 26 -> 26, of which waited for: 12 -> 13; matrix products, arithmetic and copies ran while one was open for 2% -> 2% of each run, Pallas kernels for 23% -> 24%
where the time goes in v3:
time: 128 us; the launch traced here: 127 us
  starting transfers between devices  45.9 us (36%)
  waiting for transfers between devices  44 us (34%)
  Pallas kernels  32.5 us (25%)
  local copies, waits for them, and re-layouts  2.53 us (2%)
  other arithmetic  2.08 us (2%)
    ppermute x25, waiting for transfers between devices, send(): return lax.ppermute(x, AXES, perm)  39.7 us
    ppermute x25, starting transfers between devices, send(): return lax.ppermute(x, AXES, perm)  36.8 us
    pallas_call x3, Pallas kernels, finish(): pl.pallas_call(functools.partial(finish_kernel, [(block[0], block[1], blo...  12.6 us
    pallas_call x3, Pallas kernels, pack(): pl.pallas_call(functools.partial(pack_kernel, messages), out_shape=[jax.S...  11.2 us
    all_to_all x1, starting transfers between devices, per_device(): lax.all_to_all(extras, 'tp', split_axis=0, concat_axis=0, tiled=True)  9.04 us
    pallas_call x1, Pallas kernels, squares(): pl.pallas_call(squares_kernel, out_shape=[jax.ShapeDtypeStruct((1, width)...  6.52 us
    all_to_all x1, waiting for transfers between devices, per_device(): lax.all_to_all(extras, 'tp', split_axis=0, concat_axis=0, tiled=True)  4.29 us
  transfers between devices with their start and end apart: 26, of which 13 were waited for; matrix products, arithmetic and copies ran while one was open for 2% of the time, Pallas kernels for 24%

profile of v3, /device:TPU:27, one launch (start us, length us, event | category | flops | bytes accessed | tf_op | source)
XLA Modules:
  0.0 127.4 jit_solution(16355356791889349710)
XLA Ops:
  0.0 1.8 %collective-permute-start = (bf16[64,128]{1,0:T(8,128)(2,1)}, bf16[64,128]{1,0:T(8,128)(2,1)S(1)}, u32[]{:S(2)}, u32[]{:S(2)}) collective-permute-start(bf16[64,128]{1,0:T(8,128)(2,1)} %bitcast.1), channel_id=1, source_target_pairs={{0,8},{1,9},{2,10},{3,11},{4,12},{5,13},{6,14},{7,15},{8,0},{9,1},... | collective-permute-start | bytes 49160 | tf_op jit(solution)/shard_map/ppermute | solution.py:42
  1.9 1.2 collective-permute-start.1
  3.0 3.9 %pack.3 = (bf16[2,2048,128]{2,1,0:T(8,128)(2,1)}, bf16[2,2048,128]{2,1,0:T(8,128)(2,1)}, bf16[2,2048,128]{2,1,0:T(8,128)(2,1)}) custom-call(s32[16,13]{1,0:T(8,128)} %tcb.13, bf16[2048,1664]{1,0:T(8,128)(2,1)} %w.3), custom_call_target="tpu_custom_call" | custom-call | bytes 6291456 | tf_op jit(solution)/shard_map/pack/pallas_call | solution.py:94
  7.0 0.5 collective-permute-start.2
  7.5 1.6 %collective-permute-start.3 = (bf16[16,1664]{1,0:T(8,128)(2,1)S(1)}, bf16[16,1664]{1,0:T(8,128)(2,1)S(1)}, u32[]{:S(2)}, u32[]{:S(2)}) collective-permute-start(bf16[16,1664]{1,0:T(8,128)(2,1)S(1)} %pad_maximum_fusion.5), channel_id=1, source_target_pairs={{0,32},{1,33},{2,34},{3,35},{4,36},{5,37},{6,38},{7,39},{8,40},{9,... | collective-permute-start | bytes 159752 | tf_op jit(solution)/shard_map/ppermute | solution.py:42
  9.1 0.7 collective-permute-done.2
  9.8 0.8 collective-permute-done.3
  10.6 1.1 collective-permute-start.4
  11.8 3.3 %collective-permute-done.4 = bf16[64,512]{1,0:T(8,128)(2,1)S(1)} collective-permute-done((bf16[64,512]{1,0:T(8,128)(2,1)S(1)}, bf16[64,512]{1,0:T(8,128)(2,1)S(1)}, u32[]{:S(2)}, u32[]{:S(2)}) %collective-permute-start.4) | collective-permute-done | bytes 65568 | tf_op jit(solution)/shard_map/ppermute | solution.py:42
  15.1 1.1 collective-permute-start.9
  16.2 0.4 collective-permute-start.10
  16.6 3.6 %collective-permute-start.6 = (bf16[32,1664]{1,0:T(8,128)(2,1)S(1)}, bf16[32,1664]{1,0:T(8,128)(2,1)S(1)}, u32[]{:S(2)}, u32[]{:S(2)}) collective-permute-start(bf16[32,1664]{1,0:T(8,128)(2,1)S(1)} %pad_maximum_fusion.3), channel_id=1, source_target_pairs={{0,96},{1,97},{2,98},{3,99},{4,100},{5,101},{6,102},{7,103},{8,104... | collective-permute-start | bytes 319496 | tf_op jit(solution)/shard_map/ppermute | solution.py:42
  20.2 4.7 %collective-permute-start.5 = (bf16[64,1024]{1,0:T(8,128)(2,1)S(1)}, bf16[64,1024]{1,0:T(8,128)(2,1)S(1)}, u32[]{:S(2)}, u32[]{:S(2)}) collective-permute-start(bf16[64,1024]{1,0:T(8,128)(2,1)S(1)} %pad_maximum_fusion.2), channel_id=1, source_target_pairs={{0,1},{1,0},{2,3},{3,2},{4,5},{5,4},{6,7},{7,6},{8,9},{9,8},{10,11... | collective-permute-start | bytes 393224 | tf_op jit(solution)/shard_map/ppermute | solution.py:42
  24.8 0.7 pad_maximum_fusion.1.b_rel
  25.5 0.3 collective-permute-done.5
  25.8 0.7 pad_maximum_fusion.a_rel
  26.5 6.5 %column_squares.1 = (f32[1,1664]{1,0:T(1,128)}, bf16[2048,64]{1,0:T(8,128)(2,1)}, bf16[64,1664]{1,0:T(8,128)(2,1)}) custom-call(bf16[2048,1664]{1,0:T(8,128)(2,1)} %w.3, bf16[64,2048]{1,0:T(8,128)(2,1)} %pad_maximum_fusion.a_rel, bf16[64,1664]{1,0:T(8,128)(2,1)} %pad_maximum_fusion.1.b_rel), custom_call_target="tpu_custom_call" | custom-call | flops 436207616 | bytes 6815744 | tf_op jit(solution)/shard_map/column_squares/pallas_call | solution.py:146
  33.1 0.4 collective-permute-start.7
  33.5 3.5 %pack.4 = (bf16[2,2048,128]{2,1,0:T(8,128)(2,1)}, bf16[2,2048,128]{2,1,0:T(8,128)(2,1)}) custom-call(s32[16,13]{1,0:T(8,128)} %tcb.13, bf16[2048,1664]{1,0:T(8,128)(2,1)} %w.3), custom_call_target="tpu_custom_call" | custom-call | bytes 4194304 | tf_op jit(solution)/shard_map/pack/pallas_call | solution.py:94
  37.0 1.6 %collective-permute-done.10.refs_6_ = bf16[2,2048,128]{2,1,0:T(8,128)(2,1)S(1)} collective-permute-done((bf16[2,2048,128]{2,1,0:T(8,128)(2,1)}, bf16[2,2048,128]{2,1,0:T(8,128)(2,1)S(1)}, u32[]{:S(2)}, u32[]{:S(2)}) %collective-permute-start.10) | collective-permute-done | bytes 1048608 | tf_op jit(solution)/shard_map/ppermute | solution.py:42
  38.8 4.4 %collective-permute-start.21 = (bf16[2,2048,128]{2,1,0:T(8,128)(2,1)S(1)}, bf16[2,2048,128]{2,1,0:T(8,128)(2,1)}, u32[]{:S(2)}, u32[]{:S(2)}) collective-permute-start(bf16[2,2048,128]{2,1,0:T(8,128)(2,1)S(1)} %collective-permute-done.8.refs_2_), channel_id=1, source_target_pairs={{0,1},{1,0},{2,3},{3,2},{4,5},{5,4},{6,7},{7,6},{8,9},{9,8},{10,11... | collective-permute-start | bytes 3145736 | tf_op jit(solution)/shard_map/ppermute | solution.py:42
  43.2 1.5 %collective-permute-start.11 = (f32[1,1664]{1,0:T(1,128)S(1)}, f32[1,1664]{1,0:T(1,128)S(1)}, u32[]{:S(2)}, u32[]{:S(2)}) collective-permute-start(f32[1,1664]{1,0:T(1,128)S(1)} %add.9), channel_id=1, source_target_pairs={{0,32},{1,33},{2,34},{3,35},{4,36},{5,37},{6,38},{7,39},{8,40},{9,... | collective-permute-start | bytes 19976 | tf_op jit(solution)/shard_map/ppermute | solution.py:42
  44.7 1.0 collective-permute-done.11
  45.7 3.7 %collective-permute-start.12 = (f32[1,1664]{1,0:T(1,128)S(1)}, f32[1,1664]{1,0:T(1,128)S(1)}, u32[]{:S(2)}, u32[]{:S(2)}) collective-permute-start(f32[1,1664]{1,0:T(1,128)S(1)} %add.10), channel_id=1, source_target_pairs={{0,96},{1,97},{2,98},{3,99},{4,100},{5,101},{6,102},{7,103},{8,104... | collective-permute-start | bytes 19976 | tf_op jit(solution)/shard_map/ppermute | solution.py:42
  49.4 0.6 broadcast_in_dim.3.mag
  50.0 0.8 collective-permute-done.12
  50.8 0.6 add.11.sq
  51.4 2.1 %pack_extras.1 = bf16[16,80,128]{2,1,0:T(8,128)(2,1)} custom-call(s32[16,13]{1,0:T(8,128)} %tcb.13, bf16[64,1664]{1,0:T(8,128)(2,1)} %get-tuple-element.57.b, f32[1,1664]{1,0:T(1,128)} %add.11.sq, f32[1,1664]{1,0:T(1,128)} %broadcast_in_dim.3.mag), custom_call_target="tpu_custom_call" | custom-call | tf_op jit(solution)/shard_map/pack_extras/pallas_call | solution.py:187
  53.5 9.0 %all-to-all-start = ((bf16[16,80,128]{2,1,0:T(8,128)(2,1)}), bf16[16,80,128]{2,1,0:T(8,128)(2,1)S(1)}, u32[]{:S(2)}, u32[]{:S(2)}) async-start(bf16[16,80,128]{2,1,0:T(8,128)(2,1)} %pack_extras.1), calls=%async_computation | async-start | bytes 655360 | tf_op jit(solution)/shard_map/all_to_all | solution.py:302
  62.5 0.4 collective-permute-start.22
  63.0 3.9 %pack.5 = (bf16[1,2048,128]{2,1,0:T(8,128)(2,1)}, bf16[1,2048,128]{2,1,0:T(8,128)(2,1)}, bf16[1,2048,128]{2,1,0:T(8,128)(2,1)}, bf16[1,2048,128]{2,1,0:T(8,128)(...) custom-call(s32[16,13]{1,0:T(8,128)} %tcb.13, bf16[2048,1664]{1,0:T(8,128)(2,1)} %w.3), custom_call_target="tpu_custom_call" | custom-call | bytes 6291456 | tf_op jit(solution)/shard_map/pack/pallas_call | solution.py:94
  67.0 4.3 %all-to-all-done.extras = bf16[16,80,128]{2,1,0:T(8,128)(2,1)S(1)} async-done(((bf16[16,80,128]{2,1,0:T(8,128)(2,1)}), bf16[16,80,128]{2,1,0:T(8,128)(2,1)S(1)}, u32[]{:S(2)}, u32[]{:S(2)}) %all-to-all-start) | async-done | bytes 327712 | tf_op jit(solution)/shard_map/all_to_all | solution.py:302
  71.3 0.4 collective-permute-start.20
  71.8 1.4 %collective-permute-start.17 = (bf16[1,2048,128]{2,1,0:T(8,128)(2,1)}, bf16[1,2048,128]{2,1,0:T(8,128)(2,1)S(1)}, u32[]{:S(2)}, u32[]{:S(2)}) collective-permute-start(bf16[1,2048,128]{2,1,0:T(8,128)(2,1)} %get-tuple-element.79), channel_id=1, source_target_pairs={{0,10},{1,11},{2,12},{3,13},{4,14},{5,15},{6,8},{7,9},{8,2},{9,3},... | collective-permute-start | bytes 1572872 | tf_op jit(solution)/shard_map/ppermute | solution.py:42
  73.1 2.5 %collective-permute-start.18 = (bf16[1,2048,128]{2,1,0:T(8,128)(2,1)}, bf16[1,2048,128]{2,1,0:T(8,128)(2,1)}, u32[]{:S(2)}, u32[]{:S(2)}) collective-permute-start(bf16[1,2048,128]{2,1,0:T(8,128)(2,1)} %get-tuple-element.80), channel_id=1, source_target_pairs={{0,14},{1,15},{2,8},{3,9},{4,10},{5,11},{6,12},{7,13},{8,6},{9,7},... | collective-permute-start | bytes 1572872 | tf_op jit(solution)/shard_map/ppermute | solution.py:42
  75.6 0.5 collective-permute-start.19
  76.1 11.5 %collective-permute-done.17.refs_0_ = bf16[1,2048,128]{2,1,0:T(8,128)(2,1)S(1)} collective-permute-done((bf16[1,2048,128]{2,1,0:T(8,128)(2,1)}, bf16[1,2048,128]{2,1,0:T(8,128)(2,1)S(1)}, u32[]{:S(2)}, u32[]{:S(2)}) %collective-permute-start.17) | collective-permute-done | bytes 524320 | tf_op jit(solution)/shard_map/ppermute | solution.py:42
  87.6 4.5 %collective-permute-start.14 = (bf16[1,2048,128]{2,1,0:T(8,128)(2,1)}, bf16[1,2048,128]{2,1,0:T(8,128)(2,1)S(1)}, u32[]{:S(2)}, u32[]{:S(2)}) collective-permute-start(bf16[1,2048,128]{2,1,0:T(8,128)(2,1)} %get-tuple-element.76), channel_id=1, source_target_pairs={{0,11},{1,10},{2,13},{3,12},{4,15},{5,14},{6,9},{7,8},{8,3},{9,2},... | collective-permute-start | bytes 1572872 | tf_op jit(solution)/shard_map/ppermute | solution.py:42
  92.2 0.9 copy-done.7
  93.1 1.0 copy-done.8
  94.1 0.7 collective-permute-start.16
  94.8 6.1 %finish.3.refs_3_ = bf16[2048,1664]{1,0:T(8,128)(2,1)} custom-call(s32[16,13]{1,0:T(8,128)} %tcb.13, bf16[2048,64]{1,0:T(8,128)(2,1)} %get-tuple-element.56.a, bf16[16,80,128]{2,1,0:T(8,128)(2,1)} %copy-done, bf16[2,2048,128]{2,1,0:T(8,128)(2,1)} %get-tuple-element.82.refs_0_, bf16[2,2048,128]{2,1,0:T(8,128)(2,1)} %copy-done.7, ...), custom_call_target="tpu_custom_call" | custom-call | flops 335544320 | bytes 10485760 | tf_op jit(solution)/shard_map/finish/pallas_call | solution.py:247
  101.0 0.2 collective-permute-done.19.refs_2_
  101.2 4.0 %finish.4.refs_3_ = bf16[2048,1664]{1,0:T(8,128)(2,1)} custom-call(s32[16,13]{1,0:T(8,128)} %tcb.13, bf16[2048,64]{1,0:T(8,128)(2,1)} %get-tuple-element.56.a, bf16[16,80,128]{2,1,0:T(8,128)(2,1)} %copy-done, bf16[1,2048,128]{2,1,0:T(8,128)(2,1)} %copy-done.9, bf16[1,2048,128]{2,1,0:T(8,128)(2,1)} %collective-permute-done.18.refs_1_, ...), custom_call_target="tpu_custom_call", output_to_operand_aliasing={{}: (6, {})} | custom-call | flops 100663296 | bytes 3145728 | tf_op jit(solution)/shard_map/finish/pallas_call | solution.py:247
  105.2 7.5 %collective-permute-done.14.refs_0_ = bf16[1,2048,128]{2,1,0:T(8,128)(2,1)S(1)} collective-permute-done((bf16[1,2048,128]{2,1,0:T(8,128)(2,1)}, bf16[1,2048,128]{2,1,0:T(8,128)(2,1)S(1)}, u32[]{:S(2)}, u32[]{:S(2)}) %collective-permute-start.14) | collective-permute-done | bytes 524320 | tf_op jit(solution)/shard_map/ppermute | solution.py:42
  112.7 9.9 %collective-permute-done.15.refs_1_ = bf16[1,2048,128]{2,1,0:T(8,128)(2,1)S(1)} collective-permute-done((bf16[1,2048,128]{2,1,0:T(8,128)(2,1)}, bf16[1,2048,128]{2,1,0:T(8,128)(2,1)S(1)}, u32[]{:S(2)}, u32[]{:S(2)}) %collective-permute-start.15) | collective-permute-done | bytes 524320 | tf_op jit(solution)/shard_map/ppermute | solution.py:42
  122.7 2.1 %collective-permute-done.16.refs_2_ = bf16[1,2048,128]{2,1,0:T(8,128)(2,1)S(1)} collective-permute-done((bf16[1,2048,128]{2,1,0:T(8,128)(2,1)}, bf16[1,2048,128]{2,1,0:T(8,128)(2,1)S(1)}, u32[]{:S(2)}, u32[]{:S(2)}) %collective-permute-start.16) | collective-permute-done | bytes 524320 | tf_op jit(solution)/shard_map/ppermute | solution.py:42
  124.7 2.5 %finish.5 = bf16[2048,1664]{1,0:T(8,128)(2,1)} custom-call(s32[16,13]{1,0:T(8,128)S(1)} %copy-done.3, bf16[2048,64]{1,0:T(8,128)(2,1)S(1)} %copy-done.2, bf16[16,80,128]{2,1,0:T(8,128)(2,1)S(1)} %copy-done.1, bf16[1,2048,128]{2,1,0:T(8,128)(2,1)S(1)} %collective-permute-done.14.refs_0_, ...), custom_call_target="tpu_custom_call", output_to_operand_aliasing={{}: (6, {})} | custom-call | flops 100663296 | bytes 3145728 | tf_op jit(solution)/shard_map/finish/pallas_call | solution.py:247
  (51 shorter events, 0.7 us)
Async XLA Ops:
  0.0 6.9 %copy-start.11 = (bf16[128,64]{0,1:T(8,128)(2,1)S(1)}, bf16[128,64]{0,1:T(8,128)(2,1)}, u32[]{:S(2)}) copy-start(bf16[128,64]{0,1:T(8,128)(2,1)} %param.6) | copy-start | bytes 49156
  0.0 6.9 %copy-start.10 = (bf16[8,1664]{1,0:T(8,128)(2,1)S(1)}, bf16[8,1664]{1,0:T(8,128)(2,1)}, u32[]{:S(2)}) copy-start(bf16[8,1664]{1,0:T(8,128)(2,1)} %param.7) | copy-start | bytes 79876
  0.0 6.9 %collective-permute-start = (bf16[64,128]{1,0:T(8,128)(2,1)}, bf16[64,128]{1,0:T(8,128)(2,1)S(1)}, u32[]{:S(2)}, u32[]{:S(2)}) collective-permute-start(bf16[64,128]{1,0:T(8,128)(2,1)} %bitcast.1), channel_id=1, source_target_pairs={{0,8},{1,9},{2,10},{3,11},{4,12},{5,13},{6,14},{7,15},{8,0},{9,1},... | collective-permute-start | bytes 49160 | tf_op jit(solution)/shard_map/ppermute | solution.py:42
  1.9 5.1 %collective-permute-start.1 = (bf16[8,1664]{1,0:T(8,128)(2,1)}, bf16[8,1664]{1,0:T(8,128)(2,1)S(1)}, u32[]{:S(2)}, u32[]{:S(2)}) collective-permute-start(bf16[8,1664]{1,0:T(8,128)(2,1)} %param.7), channel_id=1, source_target_pairs={{0,16},{1,17},{2,18},{3,19},{4,20},{5,21},{6,22},{7,23},{8,24},{9,... | collective-permute-start | bytes 79880 | tf_op jit(solution)/shard_map/ppermute | solution.py:42
  7.0 2.8 %collective-permute-start.2 = (bf16[64,256]{1,0:T(8,128)(2,1)S(1)}, bf16[64,256]{1,0:T(8,128)(2,1)S(1)}, u32[]{:S(2)}, u32[]{:S(2)}) collective-permute-start(bf16[64,256]{1,0:T(8,128)(2,1)S(1)} %pad_maximum_fusion.6), channel_id=1, source_target_pairs={{0,2},{1,3},{2,0},{3,1},{4,6},{5,7},{6,4},{7,5},{8,10},{9,11},{10,... | collective-permute-start | bytes 98312 | tf_op jit(solution)/shard_map/ppermute | solution.py:42
  7.5 3.2 %collective-permute-start.3 = (bf16[16,1664]{1,0:T(8,128)(2,1)S(1)}, bf16[16,1664]{1,0:T(8,128)(2,1)S(1)}, u32[]{:S(2)}, u32[]{:S(2)}) collective-permute-start(bf16[16,1664]{1,0:T(8,128)(2,1)S(1)} %pad_maximum_fusion.5), channel_id=1, source_target_pairs={{0,32},{1,33},{2,34},{3,35},{4,36},{5,37},{6,38},{7,39},{8,40},{9,... | collective-permute-start | bytes 159752 | tf_op jit(solution)/shard_map/ppermute | solution.py:42
  10.6 4.4 %collective-permute-start.4 = (bf16[64,512]{1,0:T(8,128)(2,1)S(1)}, bf16[64,512]{1,0:T(8,128)(2,1)S(1)}, u32[]{:S(2)}, u32[]{:S(2)}) collective-permute-start(bf16[64,512]{1,0:T(8,128)(2,1)S(1)} %pad_maximum_fusion.4), channel_id=1, source_target_pairs={{0,6},{1,7},{2,4},{3,5},{4,2},{5,3},{6,0},{7,1},{8,14},{9,15},{10,... | collective-permute-start | bytes 196616 | tf_op jit(solution)/shard_map/ppermute | solution.py:42
  11.8 25.2 %collective-permute-start.8 = (bf16[2,2048,128]{2,1,0:T(8,128)(2,1)}, bf16[2,2048,128]{2,1,0:T(8,128)(2,1)S(1)}, u32[]{:S(2)}, u32[]{:S(2)}) collective-permute-start(bf16[2,2048,128]{2,1,0:T(8,128)(2,1)} %get-tuple-element.59), channel_id=1, source_target_pairs={{0,8},{1,9},{2,10},{3,11},{4,12},{5,13},{6,14},{7,15},{8,0},{9,1},... | collective-permute-start | bytes 3145736 | tf_op jit(solution)/shard_map/ppermute | solution.py:42
  15.1 22.0 %collective-permute-start.9 = (bf16[2,2048,128]{2,1,0:T(8,128)(2,1)}, bf16[2,2048,128]{2,1,0:T(8,128)(2,1)S(1)}, u32[]{:S(2)}, u32[]{:S(2)}) collective-permute-start(bf16[2,2048,128]{2,1,0:T(8,128)(2,1)} %get-tuple-element.60), channel_id=1, source_target_pairs={{0,2},{1,3},{2,4},{3,5},{4,6},{5,7},{6,0},{7,1},{8,10},{9,11},{10,... | collective-permute-start | bytes 3145736 | tf_op jit(solution)/shard_map/ppermute | solution.py:42
  16.2 22.4 %collective-permute-start.10 = (bf16[2,2048,128]{2,1,0:T(8,128)(2,1)}, bf16[2,2048,128]{2,1,0:T(8,128)(2,1)S(1)}, u32[]{:S(2)}, u32[]{:S(2)}) collective-permute-start(bf16[2,2048,128]{2,1,0:T(8,128)(2,1)} %get-tuple-element.61), channel_id=1, source_target_pairs={{0,6},{1,7},{2,0},{3,1},{4,2},{5,3},{6,4},{7,5},{8,14},{9,15},{10,... | collective-permute-start | bytes 3145736 | tf_op jit(solution)/shard_map/ppermute | solution.py:42
  16.6 8.2 %collective-permute-start.6 = (bf16[32,1664]{1,0:T(8,128)(2,1)S(1)}, bf16[32,1664]{1,0:T(8,128)(2,1)S(1)}, u32[]{:S(2)}, u32[]{:S(2)}) collective-permute-start(bf16[32,1664]{1,0:T(8,128)(2,1)S(1)} %pad_maximum_fusion.3), channel_id=1, source_target_pairs={{0,96},{1,97},{2,98},{3,99},{4,100},{5,101},{6,102},{7,103},{8,104... | collective-permute-start | bytes 319496 | tf_op jit(solution)/shard_map/ppermute | solution.py:42
  20.2 5.6 %collective-permute-start.5 = (bf16[64,1024]{1,0:T(8,128)(2,1)S(1)}, bf16[64,1024]{1,0:T(8,128)(2,1)S(1)}, u32[]{:S(2)}, u32[]{:S(2)}) collective-permute-start(bf16[64,1024]{1,0:T(8,128)(2,1)S(1)} %pad_maximum_fusion.2), channel_id=1, source_target_pairs={{0,1},{1,0},{2,3},{3,2},{4,5},{5,4},{6,7},{7,6},{8,9},{9,8},{10,11... | collective-permute-start | bytes 393224 | tf_op jit(solution)/shard_map/ppermute | solution.py:42
  26.5 22.8 %copy-start.12 = (f32[1664]{0:T(1024)S(1)}, f32[1664]{0:T(1024)}, u32[]{:S(2)}) copy-start(f32[1664]{0:T(1024)} %param.8) | copy-start | bytes 19972
  33.1 3.9 %copy-start.13 = (f32[1,1664]{1,0:T(1,128)S(1)}, f32[1,1664]{1,0:T(1,128)}, u32[]{:S(2)}) copy-start(f32[1,1664]{1,0:T(1,128)} %get-tuple-element.58) | copy-start | bytes 19972
  33.1 3.9 %collective-permute-start.7 = (f32[1,1664]{1,0:T(1,128)}, f32[1,1664]{1,0:T(1,128)S(1)}, u32[]{:S(2)}, u32[]{:S(2)}) collective-permute-start(f32[1,1664]{1,0:T(1,128)} %get-tuple-element.58), channel_id=1, source_target_pairs={{0,16},{1,17},{2,18},{3,19},{4,20},{5,21},{6,22},{7,23},{8,24},{9,... | collective-permute-start | bytes 19976 | tf_op jit(solution)/shard_map/ppermute | solution.py:42
  37.0 57.8 %copy-start.4 = (bf16[2,2048,128]{2,1,0:T(8,128)(2,1)}, bf16[2,2048,128]{2,1,0:T(8,128)(2,1)S(1)}, u32[]{:S(2)}) copy-start(bf16[2,2048,128]{2,1,0:T(8,128)(2,1)S(1)} %collective-permute-done.8.refs_2_) | copy-start | bytes 3145732
  37.0 57.8 %copy-start.5 = (bf16[2,2048,128]{2,1,0:T(8,128)(2,1)}, bf16[2,2048,128]{2,1,0:T(8,128)(2,1)S(1)}, u32[]{:S(2)}) copy-start(bf16[2,2048,128]{2,1,0:T(8,128)(2,1)S(1)} %collective-permute-done.9.refs_4_) | copy-start | bytes 3145732
  38.6 53.5 %copy-start.6 = (bf16[2,2048,128]{2,1,0:T(8,128)(2,1)}, bf16[2,2048,128]{2,1,0:T(8,128)(2,1)S(1)}, u32[]{:S(2)}) copy-start(bf16[2,2048,128]{2,1,0:T(8,128)(2,1)S(1)} %collective-permute-done.10.refs_6_) | copy-start | bytes 3145732
  38.6 32.6 %collective-permute-start.13 = (bf16[2,2048,128]{2,1,0:T(8,128)(2,1)}, bf16[2,2048,128]{2,1,0:T(8,128)(2,1)}, u32[]{:S(2)}, u32[]{:S(2)}) collective-permute-start(bf16[2,2048,128]{2,1,0:T(8,128)(2,1)} %get-tuple-element.66), channel_id=1, source_target_pairs={{0,12},{1,13},{2,14},{3,15},{4,8},{5,9},{6,10},{7,11},{8,4},{9,5},... | collective-permute-start | bytes 3145736 | tf_op jit(solution)/shard_map/ppermute | solution.py:42
  38.8 33.0 %collective-permute-start.21 = (bf16[2,2048,128]{2,1,0:T(8,128)(2,1)S(1)}, bf16[2,2048,128]{2,1,0:T(8,128)(2,1)}, u32[]{:S(2)}, u32[]{:S(2)}) collective-permute-start(bf16[2,2048,128]{2,1,0:T(8,128)(2,1)S(1)} %collective-permute-done.8.refs_2_), channel_id=1, source_target_pairs={{0,1},{1,0},{2,3},{3,2},{4,5},{5,4},{6,7},{7,6},{8,9},{9,8},{10,11... | collective-permute-start | bytes 3145736 | tf_op jit(solution)/shard_map/ppermute | solution.py:42
  43.2 2.5 %collective-permute-start.11 = (f32[1,1664]{1,0:T(1,128)S(1)}, f32[1,1664]{1,0:T(1,128)S(1)}, u32[]{:S(2)}, u32[]{:S(2)}) collective-permute-start(f32[1,1664]{1,0:T(1,128)S(1)} %add.9), channel_id=1, source_target_pairs={{0,32},{1,33},{2,34},{3,35},{4,36},{5,37},{6,38},{7,39},{8,40},{9,... | collective-permute-start | bytes 19976 | tf_op jit(solution)/shard_map/ppermute | solution.py:42
  45.7 5.1 %collective-permute-start.12 = (f32[1,1664]{1,0:T(1,128)S(1)}, f32[1,1664]{1,0:T(1,128)S(1)}, u32[]{:S(2)}, u32[]{:S(2)}) collective-permute-start(f32[1,1664]{1,0:T(1,128)S(1)} %add.10), channel_id=1, source_target_pairs={{0,96},{1,97},{2,98},{3,99},{4,100},{5,101},{6,102},{7,103},{8,104... | collective-permute-start | bytes 19976 | tf_op jit(solution)/shard_map/ppermute | solution.py:42
  53.5 17.8 %all-to-all-start = ((bf16[16,80,128]{2,1,0:T(8,128)(2,1)}), bf16[16,80,128]{2,1,0:T(8,128)(2,1)S(1)}, u32[]{:S(2)}, u32[]{:S(2)}) async-start(bf16[16,80,128]{2,1,0:T(8,128)(2,1)} %pack_extras.1), calls=%async_computation | async-start | bytes 655360 | tf_op jit(solution)/shard_map/all_to_all | solution.py:302
  62.5 10.6 %collective-permute-start.22 = (bf16[2,2048,128]{2,1,0:T(8,128)(2,1)S(1)}, bf16[2,2048,128]{2,1,0:T(8,128)(2,1)}, u32[]{:S(2)}, u32[]{:S(2)}) collective-permute-start(bf16[2,2048,128]{2,1,0:T(8,128)(2,1)S(1)} %collective-permute-done.9.refs_4_), channel_id=1, source_target_pairs={{0,1},{1,0},{2,3},{3,2},{4,5},{5,4},{6,7},{7,6},{8,9},{9,8},{10,11... | collective-permute-start | bytes 3145736 | tf_op jit(solution)/shard_map/ppermute | solution.py:42
  62.9 12.7 %collective-permute-start.23 = (bf16[2,2048,128]{2,1,0:T(8,128)(2,1)S(1)}, bf16[2,2048,128]{2,1,0:T(8,128)(2,1)}, u32[]{:S(2)}, u32[]{:S(2)}) collective-permute-start(bf16[2,2048,128]{2,1,0:T(8,128)(2,1)S(1)} %collective-permute-done.10.refs_6_), channel_id=1, source_target_pairs={{0,1},{1,0},{2,3},{3,2},{4,5},{5,4},{6,7},{7,6},{8,9},{9,8},{10,11... | collective-permute-start | bytes 3145736 | tf_op jit(solution)/shard_map/ppermute | solution.py:42
  71.2 23.6 %copy-start = (bf16[16,80,128]{2,1,0:T(8,128)(2,1)}, bf16[16,80,128]{2,1,0:T(8,128)(2,1)S(1)}, u32[]{:S(2)}) copy-start(bf16[16,80,128]{2,1,0:T(8,128)(2,1)S(1)} %all-to-all-done.extras) | copy-start | bytes 983044
  71.3 20.9 %collective-permute-start.20 = (bf16[2,2048,128]{2,1,0:T(8,128)(2,1)}, bf16[2,2048,128]{2,1,0:T(8,128)(2,1)S(1)}, u32[]{:S(2)}, u32[]{:S(2)}) collective-permute-start(bf16[2,2048,128]{2,1,0:T(8,128)(2,1)} %get-tuple-element.82.refs_0_), channel_id=1, source_target_pairs={{0,1},{1,0},{2,3},{3,2},{4,5},{5,4},{6,7},{7,6},{8,9},{9,8},{10,11... | collective-permute-start | bytes 3145736 | tf_op jit(solution)/shard_map/ppermute | solution.py:42
  71.6 21.5 %collective-permute-start.24 = (bf16[2,2048,128]{2,1,0:T(8,128)(2,1)}, bf16[2,2048,128]{2,1,0:T(8,128)(2,1)S(1)}, u32[]{:S(2)}, u32[]{:S(2)}) collective-permute-start(bf16[2,2048,128]{2,1,0:T(8,128)(2,1)} %collective-permute-done.13.refs_8_), channel_id=1, source_target_pairs={{0,1},{1,0},{2,3},{3,2},{4,5},{5,4},{6,7},{7,6},{8,9},{9,8},{10,11... | collective-permute-start | bytes 3145736 | tf_op jit(solution)/shard_map/ppermute | solution.py:42
  71.8 15.9 %collective-permute-start.17 = (bf16[1,2048,128]{2,1,0:T(8,128)(2,1)}, bf16[1,2048,128]{2,1,0:T(8,128)(2,1)S(1)}, u32[]{:S(2)}, u32[]{:S(2)}) collective-permute-start(bf16[1,2048,128]{2,1,0:T(8,128)(2,1)} %get-tuple-element.79), channel_id=1, source_target_pairs={{0,10},{1,11},{2,12},{3,13},{4,14},{5,15},{6,8},{7,9},{8,2},{9,3},... | collective-permute-start | bytes 1572872 | tf_op jit(solution)/shard_map/ppermute | solution.py:42
  73.1 27.9 %collective-permute-start.18 = (bf16[1,2048,128]{2,1,0:T(8,128)(2,1)}, bf16[1,2048,128]{2,1,0:T(8,128)(2,1)}, u32[]{:S(2)}, u32[]{:S(2)}) collective-permute-start(bf16[1,2048,128]{2,1,0:T(8,128)(2,1)} %get-tuple-element.80), channel_id=1, source_target_pairs={{0,14},{1,15},{2,8},{3,9},{4,10},{5,11},{6,12},{7,13},{8,6},{9,7},... | collective-permute-start | bytes 1572872 | tf_op jit(solution)/shard_map/ppermute | solution.py:42
  75.6 25.5 %collective-permute-start.19 = (bf16[1,2048,128]{2,1,0:T(8,128)(2,1)}, bf16[1,2048,128]{2,1,0:T(8,128)(2,1)}, u32[]{:S(2)}, u32[]{:S(2)}) collective-permute-start(bf16[1,2048,128]{2,1,0:T(8,128)(2,1)} %get-tuple-element.81), channel_id=1, source_target_pairs={{0,4},{1,5},{2,6},{3,7},{4,0},{5,1},{6,2},{7,3},{8,12},{9,13},{10,... | collective-permute-start | bytes 1572872 | tf_op jit(solution)/shard_map/ppermute | solution.py:42
  87.6 7.2 %copy-start.9 = (bf16[1,2048,128]{2,1,0:T(8,128)(2,1)}, bf16[1,2048,128]{2,1,0:T(8,128)(2,1)S(1)}, u32[]{:S(2)}) copy-start(bf16[1,2048,128]{2,1,0:T(8,128)(2,1)S(1)} %collective-permute-done.17.refs_0_) | copy-start | bytes 1572868
  87.6 25.1 %collective-permute-start.14 = (bf16[1,2048,128]{2,1,0:T(8,128)(2,1)}, bf16[1,2048,128]{2,1,0:T(8,128)(2,1)S(1)}, u32[]{:S(2)}, u32[]{:S(2)}) collective-permute-start(bf16[1,2048,128]{2,1,0:T(8,128)(2,1)} %get-tuple-element.76), channel_id=1, source_target_pairs={{0,11},{1,10},{2,13},{3,12},{4,15},{5,14},{6,9},{7,8},{8,3},{9,2},... | collective-permute-start | bytes 1572872 | tf_op jit(solution)/shard_map/ppermute | solution.py:42
  92.1 1.0 copy-start.7
  92.1 30.5 %collective-permute-start.15 = (bf16[1,2048,128]{2,1,0:T(8,128)(2,1)}, bf16[1,2048,128]{2,1,0:T(8,128)(2,1)S(1)}, u32[]{:S(2)}, u32[]{:S(2)}) collective-permute-start(bf16[1,2048,128]{2,1,0:T(8,128)(2,1)} %get-tuple-element.77), channel_id=1, source_target_pairs={{0,15},{1,14},{2,9},{3,8},{4,11},{5,10},{6,13},{7,12},{8,7},{9,6},... | collective-permute-start | bytes 1572872 | tf_op jit(solution)/shard_map/ppermute | solution.py:42
  93.1 1.0 copy-start.8
  94.1 30.6 %collective-permute-start.16 = (bf16[1,2048,128]{2,1,0:T(8,128)(2,1)}, bf16[1,2048,128]{2,1,0:T(8,128)(2,1)S(1)}, u32[]{:S(2)}, u32[]{:S(2)}) collective-permute-start(bf16[1,2048,128]{2,1,0:T(8,128)(2,1)} %get-tuple-element.78), channel_id=1, source_target_pairs={{0,5},{1,4},{2,7},{3,6},{4,1},{5,0},{6,3},{7,2},{8,13},{9,12},{10,... | collective-permute-start | bytes 1572872 | tf_op jit(solution)/shard_map/ppermute | solution.py:42
  101.0 23.8 %copy-start.1 = (bf16[16,80,128]{2,1,0:T(8,128)(2,1)S(1)}, bf16[16,80,128]{2,1,0:T(8,128)(2,1)}, u32[]{:S(2)}) copy-start(bf16[16,80,128]{2,1,0:T(8,128)(2,1)} %copy-done) | copy-start | bytes 983044
  101.0 23.8 %copy-start.2 = (bf16[2048,64]{1,0:T(8,128)(2,1)S(1)}, bf16[2048,64]{1,0:T(8,128)(2,1)}, u32[]{:S(2)}) copy-start(bf16[2048,64]{1,0:T(8,128)(2,1)} %get-tuple-element.56.a) | copy-start | bytes 786436
  101.0 23.7 %copy-start.3 = (s32[16,13]{1,0:T(8,128)S(1)}, s32[16,13]{1,0:T(8,128)}, u32[]{:S(2)}) copy-start(s32[16,13]{1,0:T(8,128)} %tcb.13) | copy-start | bytes 2500

commit v4 on v3

--- a/solution.py
+++ b/solution.py
@@ -283,9 +283,10 @@
     a, b = gather(adapter_down_factor.T, adapter_up_factor, 0)
     a, b, head = after((a, b, head))
     direct[0] = send(head[0], tp_perm(chips[0]))
-    a, b = after(gather(a, b, 1))
-    a, b = gather(a, b, 2)
-    a, head[1:3], weight_then = after((a, head[1:3], weight))
+    a, b = gather(a, b, 1)
+    a = jnp.concatenate([a, send(a, tp_xor(A_MASKS[2]))], axis=1)
+    a, b, head[1:3], weight_then = after((a, b, head[1:3], weight))
+    b = jnp.concatenate([b, send(b, fsdp_xor(B_MASKS[2]))], axis=0)
     for n in (1, 2):
         direct[n] = send(head[n], tp_perm(chips[n]))
     a = jnp.concatenate([a, send(a, tp_xor(A_MASKS[3]))], axis=1)

time: 128 us -> 129 us (level); the launches traced: 127 us -> 127 us
  starting transfers between devices: 45.9 us -> 43.4 us
    all_to_all x1, starting transfers between devices: 9.04 us -> 7.31 us  [per_device(): lax.all_to_all(extras, 'tp', split_axis=0, concat_axis=0, tiled=True)]
  transfers between devices with their start and end apart: 26 -> 26, of which waited for: 13 -> 12; matrix products, arithmetic and copies ran while one was open for 2% -> 2% of each run, Pallas kernels for 24% -> 24%
where the time goes in v4:
time: 129 us; the launch traced here: 127 us
  waiting for transfers between devices  45 us (35%)
  starting transfers between devices  43.4 us (34%)
  Pallas kernels  33.2 us (26%)
  local copies, waits for them, and re-layouts  2.53 us (2%)
  other arithmetic  2.08 us (2%)
    ppermute x25, waiting for transfers between devices, send(): return lax.ppermute(x, AXES, perm)  40.7 us
    ppermute x25, starting transfers between devices, send(): return lax.ppermute(x, AXES, perm)  36.1 us
    pallas_call x3, Pallas kernels, finish(): pl.pallas_call(functools.partial(finish_kernel, [(block[0], block[1], blo...  12.8 us
    pallas_call x3, Pallas kernels, pack(): pl.pallas_call(functools.partial(pack_kernel, messages), out_shape=[jax.S...  11.8 us
    all_to_all x1, starting transfers between devices, per_device(): lax.all_to_all(extras, 'tp', split_axis=0, concat_axis=0, tiled=True)  7.31 us
    pallas_call x1, Pallas kernels, squares(): pl.pallas_call(squares_kernel, out_shape=[jax.ShapeDtypeStruct((1, width)...  6.52 us
    all_to_all x1, waiting for transfers between devices, per_device(): lax.all_to_all(extras, 'tp', split_axis=0, concat_axis=0, tiled=True)  4.29 us
  transfers between devices with their start and end apart: 26, of which 12 were waited for; matrix products, arithmetic and copies ran while one was open for 2% of the time, Pallas kernels for 24%

profile of v4, /device:TPU:27, one launch (start us, length us, event | category | flops | bytes accessed | tf_op | source)
XLA Modules:
  0.0 126.6 jit_solution(18082507968390158377)
XLA Ops:
  0.0 1.8 %collective-permute-start = (bf16[64,128]{1,0:T(8,128)(2,1)}, bf16[64,128]{1,0:T(8,128)(2,1)S(1)}, u32[]{:S(2)}, u32[]{:S(2)}) collective-permute-start(bf16[64,128]{1,0:T(8,128)(2,1)} %bitcast.1), channel_id=1, source_target_pairs={{0,8},{1,9},{2,10},{3,11},{4,12},{5,13},{6,14},{7,15},{8,0},{9,1},... | collective-permute-start | bytes 49160 | tf_op jit(solution)/shard_map/ppermute | solution.py:42
  1.9 1.2 collective-permute-start.1
  3.0 4.4 %pack.3 = (bf16[2,2048,128]{2,1,0:T(8,128)(2,1)}, bf16[2,2048,128]{2,1,0:T(8,128)(2,1)}, bf16[2,2048,128]{2,1,0:T(8,128)(2,1)}) custom-call(s32[16,13]{1,0:T(8,128)} %tcb.13, bf16[2048,1664]{1,0:T(8,128)(2,1)} %w.3), custom_call_target="tpu_custom_call" | custom-call | bytes 6291456 | tf_op jit(solution)/shard_map/pack/pallas_call | solution.py:94
  7.5 0.1 collective-permute-start.2
  7.6 1.7 %collective-permute-start.4 = (bf16[16,1664]{1,0:T(8,128)(2,1)S(1)}, bf16[16,1664]{1,0:T(8,128)(2,1)S(1)}, u32[]{:S(2)}, u32[]{:S(2)}) collective-permute-start(bf16[16,1664]{1,0:T(8,128)(2,1)S(1)} %pad_maximum_fusion.5), channel_id=1, source_target_pairs={{0,32},{1,33},{2,34},{3,35},{4,36},{5,37},{6,38},{7,39},{8,40},{9,... | collective-permute-start | bytes 159752 | tf_op jit(solution)/shard_map/ppermute | solution.py:42
  9.3 1.0 collective-permute-done.2
  10.4 0.5 collective-permute-done.4
  10.8 3.8 %collective-permute-done.3 = bf16[64,512]{1,0:T(8,128)(2,1)S(1)} collective-permute-done((bf16[64,512]{1,0:T(8,128)(2,1)S(1)}, bf16[64,512]{1,0:T(8,128)(2,1)S(1)}, u32[]{:S(2)}, u32[]{:S(2)}) %collective-permute-start.3) | collective-permute-done | bytes 65568 | tf_op jit(solution)/shard_map/ppermute | solution.py:42
  14.7 0.1 collective-permute-start.9
  14.8 1.5 %collective-permute-start.10 = (bf16[2,2048,128]{2,1,0:T(8,128)(2,1)}, bf16[2,2048,128]{2,1,0:T(8,128)(2,1)S(1)}, u32[]{:S(2)}, u32[]{:S(2)}) collective-permute-start(bf16[2,2048,128]{2,1,0:T(8,128)(2,1)} %get-tuple-element.59), channel_id=1, source_target_pairs={{0,6},{1,7},{2,0},{3,1},{4,2},{5,3},{6,4},{7,5},{8,14},{9,15},{10,... | collective-permute-start | bytes 3145736 | tf_op jit(solution)/shard_map/ppermute | solution.py:42
  16.2 3.9 %collective-permute-start.6 = (bf16[32,1664]{1,0:T(8,128)(2,1)S(1)}, bf16[32,1664]{1,0:T(8,128)(2,1)S(1)}, u32[]{:S(2)}, u32[]{:S(2)}) collective-permute-start(bf16[32,1664]{1,0:T(8,128)(2,1)S(1)} %pad_maximum_fusion.3), channel_id=1, source_target_pairs={{0,96},{1,97},{2,98},{3,99},{4,100},{5,101},{6,102},{7,103},{8,104... | collective-permute-start | bytes 319496 | tf_op jit(solution)/shard_map/ppermute | solution.py:42
  20.1 4.0 %collective-permute-start.5 = (bf16[64,1024]{1,0:T(8,128)(2,1)S(1)}, bf16[64,1024]{1,0:T(8,128)(2,1)S(1)}, u32[]{:S(2)}, u32[]{:S(2)}) collective-permute-start(bf16[64,1024]{1,0:T(8,128)(2,1)S(1)} %pad_maximum_fusion.2), channel_id=1, source_target_pairs={{0,1},{1,0},{2,3},{3,2},{4,5},{5,4},{6,7},{7,6},{8,9},{9,8},{10,11... | collective-permute-start | bytes 393224 | tf_op jit(solution)/shard_map/ppermute | solution.py:42
  24.1 0.7 pad_maximum_fusion.1.b_rel
  24.8 0.3 collective-permute-done.5
  25.1 0.7 pad_maximum_fusion.a_rel
  25.8 6.5 %column_squares.1 = (f32[1,1664]{1,0:T(1,128)}, bf16[2048,64]{1,0:T(8,128)(2,1)}, bf16[64,1664]{1,0:T(8,128)(2,1)}) custom-call(bf16[2048,1664]{1,0:T(8,128)(2,1)} %w.3, bf16[64,2048]{1,0:T(8,128)(2,1)} %pad_maximum_fusion.a_rel, bf16[64,1664]{1,0:T(8,128)(2,1)} %pad_maximum_fusion.1.b_rel), custom_call_target="tpu_custom_call" | custom-call | flops 436207616 | bytes 6815744 | tf_op jit(solution)/shard_map/column_squares/pallas_call | solution.py:146
  32.4 0.4 collective-permute-start.7
  32.8 3.5 %pack.4 = (bf16[2,2048,128]{2,1,0:T(8,128)(2,1)}, bf16[2,2048,128]{2,1,0:T(8,128)(2,1)}) custom-call(s32[16,13]{1,0:T(8,128)} %tcb.13, bf16[2048,1664]{1,0:T(8,128)(2,1)} %w.3), custom_call_target="tpu_custom_call" | custom-call | bytes 4194304 | tf_op jit(solution)/shard_map/pack/pallas_call | solution.py:94
  36.3 1.3 %collective-permute-done.10.refs_6_ = bf16[2,2048,128]{2,1,0:T(8,128)(2,1)S(1)} collective-permute-done((bf16[2,2048,128]{2,1,0:T(8,128)(2,1)}, bf16[2,2048,128]{2,1,0:T(8,128)(2,1)S(1)}, u32[]{:S(2)}, u32[]{:S(2)}) %collective-permute-start.10) | collective-permute-done | bytes 1048608 | tf_op jit(solution)/shard_map/ppermute | solution.py:42
  37.6 3.0 %collective-permute-start.13 = (bf16[2,2048,128]{2,1,0:T(8,128)(2,1)}, bf16[2,2048,128]{2,1,0:T(8,128)(2,1)}, u32[]{:S(2)}, u32[]{:S(2)}) collective-permute-start(bf16[2,2048,128]{2,1,0:T(8,128)(2,1)} %get-tuple-element.64), channel_id=1, source_target_pairs={{0,12},{1,13},{2,14},{3,15},{4,8},{5,9},{6,10},{7,11},{8,4},{9,5},... | collective-permute-start | bytes 3145736 | tf_op jit(solution)/shard_map/ppermute | solution.py:42
  40.6 4.2 %collective-permute-start.21 = (bf16[2,2048,128]{2,1,0:T(8,128)(2,1)S(1)}, bf16[2,2048,128]{2,1,0:T(8,128)(2,1)}, u32[]{:S(2)}, u32[]{:S(2)}) collective-permute-start(bf16[2,2048,128]{2,1,0:T(8,128)(2,1)S(1)} %collective-permute-done.8.refs_2_), channel_id=1, source_target_pairs={{0,1},{1,0},{2,3},{3,2},{4,5},{5,4},{6,7},{7,6},{8,9},{9,8},{10,11... | collective-permute-start | bytes 3145736 | tf_op jit(solution)/shard_map/ppermute | solution.py:42
  44.8 2.5 %collective-permute-done.11 = f32[1,1664]{1,0:T(1,128)S(1)} collective-permute-done((f32[1,1664]{1,0:T(1,128)S(1)}, f32[1,1664]{1,0:T(1,128)S(1)}, u32[]{:S(2)}, u32[]{:S(2)}) %collective-permute-start.11) | collective-permute-done | bytes 6688 | tf_op jit(solution)/shard_map/ppermute | solution.py:42
  47.3 2.3 %collective-permute-start.12 = (f32[1,1664]{1,0:T(1,128)S(1)}, f32[1,1664]{1,0:T(1,128)S(1)}, u32[]{:S(2)}, u32[]{:S(2)}) collective-permute-start(f32[1,1664]{1,0:T(1,128)S(1)} %add.10), channel_id=1, source_target_pairs={{0,96},{1,97},{2,98},{3,99},{4,100},{5,101},{6,102},{7,103},{8,104... | collective-permute-start | bytes 19976 | tf_op jit(solution)/shard_map/ppermute | solution.py:42
  49.6 0.6 broadcast_in_dim.3.mag
  50.2 1.3 collective-permute-done.12
  51.5 0.6 add.11.sq
  52.1 2.1 %pack_extras.1 = bf16[16,80,128]{2,1,0:T(8,128)(2,1)} custom-call(s32[16,13]{1,0:T(8,128)} %tcb.13, bf16[64,1664]{1,0:T(8,128)(2,1)} %get-tuple-element.55.b, f32[1,1664]{1,0:T(1,128)} %add.11.sq, f32[1,1664]{1,0:T(1,128)} %broadcast_in_dim.3.mag), custom_call_target="tpu_custom_call" | custom-call | tf_op jit(solution)/shard_map/pack_extras/pallas_call | solution.py:187
  54.2 7.3 %all-to-all-start = ((bf16[16,80,128]{2,1,0:T(8,128)(2,1)}), bf16[16,80,128]{2,1,0:T(8,128)(2,1)S(1)}, u32[]{:S(2)}, u32[]{:S(2)}) async-start(bf16[16,80,128]{2,1,0:T(8,128)(2,1)} %pack_extras.1), calls=%async_computation | async-start | bytes 655360 | tf_op jit(solution)/shard_map/all_to_all | solution.py:303
  61.5 0.4 collective-permute-start.22
  61.9 0.1 collective-permute-start.23
  62.0 3.9 %pack.5 = (bf16[1,2048,128]{2,1,0:T(8,128)(2,1)}, bf16[1,2048,128]{2,1,0:T(8,128)(2,1)}, bf16[1,2048,128]{2,1,0:T(8,128)(2,1)}, bf16[1,2048,128]{2,1,0:T(8,128)(...) custom-call(s32[16,13]{1,0:T(8,128)} %tcb.13, bf16[2048,1664]{1,0:T(8,128)(2,1)} %w.3), custom_call_target="tpu_custom_call" | custom-call | bytes 6291456 | tf_op jit(solution)/shard_map/pack/pallas_call | solution.py:94
  65.9 4.3 %all-to-all-done.extras = bf16[16,80,128]{2,1,0:T(8,128)(2,1)S(1)} async-done(((bf16[16,80,128]{2,1,0:T(8,128)(2,1)}), bf16[16,80,128]{2,1,0:T(8,128)(2,1)S(1)}, u32[]{:S(2)}, u32[]{:S(2)}) %all-to-all-start) | async-done | bytes 327712 | tf_op jit(solution)/shard_map/all_to_all | solution.py:303
  70.2 0.4 collective-permute-start.20
  70.6 0.1 collective-permute-start.24
  70.7 3.1 %collective-permute-start.17 = (bf16[1,2048,128]{2,1,0:T(8,128)(2,1)}, bf16[1,2048,128]{2,1,0:T(8,128)(2,1)S(1)}, u32[]{:S(2)}, u32[]{:S(2)}) collective-permute-start(bf16[1,2048,128]{2,1,0:T(8,128)(2,1)} %get-tuple-element.77), channel_id=1, source_target_pairs={{0,10},{1,11},{2,12},{3,13},{4,14},{5,15},{6,8},{7,9},{8,2},{9,3},... | collective-permute-start | bytes 1572872 | tf_op jit(solution)/shard_map/ppermute | solution.py:42
  73.8 0.7 collective-permute-start.18
  74.6 0.7 collective-permute-start.19
  75.3 11.2 %collective-permute-done.17.refs_0_ = bf16[1,2048,128]{2,1,0:T(8,128)(2,1)S(1)} collective-permute-done((bf16[1,2048,128]{2,1,0:T(8,128)(2,1)}, bf16[1,2048,128]{2,1,0:T(8,128)(2,1)S(1)}, u32[]{:S(2)}, u32[]{:S(2)}) %collective-permute-start.17) | collective-permute-done | bytes 524320 | tf_op jit(solution)/shard_map/ppermute | solution.py:42
  86.6 6.2 %collective-permute-start.14 = (bf16[1,2048,128]{2,1,0:T(8,128)(2,1)}, bf16[1,2048,128]{2,1,0:T(8,128)(2,1)S(1)}, u32[]{:S(2)}, u32[]{:S(2)}) collective-permute-start(bf16[1,2048,128]{2,1,0:T(8,128)(2,1)} %get-tuple-element.74), channel_id=1, source_target_pairs={{0,11},{1,10},{2,13},{3,12},{4,15},{5,14},{6,9},{7,8},{8,3},{9,2},... | collective-permute-start | bytes 1572872 | tf_op jit(solution)/shard_map/ppermute | solution.py:42
  92.8 0.1 collective-permute-start.15
  92.9 0.9 copy-done.7
  93.8 1.0 copy-done.8
  94.8 6.1 %finish.3.refs_3_ = bf16[2048,1664]{1,0:T(8,128)(2,1)} custom-call(s32[16,13]{1,0:T(8,128)} %tcb.13, bf16[2048,64]{1,0:T(8,128)(2,1)} %get-tuple-element.54.a, bf16[16,80,128]{2,1,0:T(8,128)(2,1)} %copy-done, bf16[2,2048,128]{2,1,0:T(8,128)(2,1)} %get-tuple-element.80.refs_0_, bf16[2,2048,128]{2,1,0:T(8,128)(2,1)} %copy-done.7, ...), custom_call_target="tpu_custom_call" | custom-call | flops 335544320 | bytes 10485760 | tf_op jit(solution)/shard_map/finish/pallas_call | solution.py:247
  101.0 3.9 %finish.4.refs_3_ = bf16[2048,1664]{1,0:T(8,128)(2,1)} custom-call(s32[16,13]{1,0:T(8,128)} %tcb.13, bf16[2048,64]{1,0:T(8,128)(2,1)} %get-tuple-element.54.a, bf16[16,80,128]{2,1,0:T(8,128)(2,1)} %copy-done, bf16[1,2048,128]{2,1,0:T(8,128)(2,1)} %copy-done.9, bf16[1,2048,128]{2,1,0:T(8,128)(2,1)} %collective-permute-done.18.refs_1_, ...), custom_call_target="tpu_custom_call", output_to_operand_aliasing={{}: (6, {})} | custom-call | flops 100663296 | bytes 3145728 | tf_op jit(solution)/shard_map/finish/pallas_call | solution.py:247
  104.9 6.8 %collective-permute-done.14.refs_0_ = bf16[1,2048,128]{2,1,0:T(8,128)(2,1)S(1)} collective-permute-done((bf16[1,2048,128]{2,1,0:T(8,128)(2,1)}, bf16[1,2048,128]{2,1,0:T(8,128)(2,1)S(1)}, u32[]{:S(2)}, u32[]{:S(2)}) %collective-permute-start.14) | collective-permute-done | bytes 524320 | tf_op jit(solution)/shard_map/ppermute | solution.py:42
  111.6 10.6 %collective-permute-done.15.refs_1_ = bf16[1,2048,128]{2,1,0:T(8,128)(2,1)S(1)} collective-permute-done((bf16[1,2048,128]{2,1,0:T(8,128)(2,1)}, bf16[1,2048,128]{2,1,0:T(8,128)(2,1)S(1)}, u32[]{:S(2)}, u32[]{:S(2)}) %collective-permute-start.15) | collective-permute-done | bytes 524320 | tf_op jit(solution)/shard_map/ppermute | solution.py:42
  122.2 1.4 %collective-permute-done.16.refs_2_ = bf16[1,2048,128]{2,1,0:T(8,128)(2,1)S(1)} collective-permute-done((bf16[1,2048,128]{2,1,0:T(8,128)(2,1)}, bf16[1,2048,128]{2,1,0:T(8,128)(2,1)S(1)}, u32[]{:S(2)}, u32[]{:S(2)}) %collective-permute-start.16) | collective-permute-done | bytes 524320 | tf_op jit(solution)/shard_map/ppermute | solution.py:42
  123.7 2.8 %finish.5 = bf16[2048,1664]{1,0:T(8,128)(2,1)} custom-call(s32[16,13]{1,0:T(8,128)S(1)} %copy-done.3, bf16[2048,64]{1,0:T(8,128)(2,1)S(1)} %copy-done.2, bf16[16,80,128]{2,1,0:T(8,128)(2,1)S(1)} %copy-done.1, bf16[1,2048,128]{2,1,0:T(8,128)(2,1)S(1)} %collective-permute-done.14.refs_0_, ...), custom_call_target="tpu_custom_call", output_to_operand_aliasing={{}: (6, {})} | custom-call | flops 100663296 | bytes 3145728 | tf_op jit(solution)/shard_map/finish/pallas_call | solution.py:247
  (51 shorter events, 0.2 us)
Async XLA Ops:
  0.0 7.4 %copy-start.11 = (bf16[128,64]{0,1:T(8,128)(2,1)S(1)}, bf16[128,64]{0,1:T(8,128)(2,1)}, u32[]{:S(2)}) copy-start(bf16[128,64]{0,1:T(8,128)(2,1)} %param.6) | copy-start | bytes 49156
  0.0 7.5 %copy-start.10 = (bf16[8,1664]{1,0:T(8,128)(2,1)S(1)}, bf16[8,1664]{1,0:T(8,128)(2,1)}, u32[]{:S(2)}) copy-start(bf16[8,1664]{1,0:T(8,128)(2,1)} %param.7) | copy-start | bytes 79876
  0.0 7.4 %collective-permute-start = (bf16[64,128]{1,0:T(8,128)(2,1)}, bf16[64,128]{1,0:T(8,128)(2,1)S(1)}, u32[]{:S(2)}, u32[]{:S(2)}) collective-permute-start(bf16[64,128]{1,0:T(8,128)(2,1)} %bitcast.1), channel_id=1, source_target_pairs={{0,8},{1,9},{2,10},{3,11},{4,12},{5,13},{6,14},{7,15},{8,0},{9,1},... | collective-permute-start | bytes 49160 | tf_op jit(solution)/shard_map/ppermute | solution.py:42
  1.9 5.6 %collective-permute-start.1 = (bf16[8,1664]{1,0:T(8,128)(2,1)}, bf16[8,1664]{1,0:T(8,128)(2,1)S(1)}, u32[]{:S(2)}, u32[]{:S(2)}) collective-permute-start(bf16[8,1664]{1,0:T(8,128)(2,1)} %param.7), channel_id=1, source_target_pairs={{0,16},{1,17},{2,18},{3,19},{4,20},{5,21},{6,22},{7,23},{8,24},{9,... | collective-permute-start | bytes 79880 | tf_op jit(solution)/shard_map/ppermute | solution.py:42
  7.5 2.8 %collective-permute-start.2 = (bf16[64,256]{1,0:T(8,128)(2,1)S(1)}, bf16[64,256]{1,0:T(8,128)(2,1)S(1)}, u32[]{:S(2)}, u32[]{:S(2)}) collective-permute-start(bf16[64,256]{1,0:T(8,128)(2,1)S(1)} %pad_maximum_fusion.6), channel_id=1, source_target_pairs={{0,2},{1,3},{2,0},{3,1},{4,6},{5,7},{6,4},{7,5},{8,10},{9,11},{10,... | collective-permute-start | bytes 98312 | tf_op jit(solution)/shard_map/ppermute | solution.py:42
  7.6 3.2 %collective-permute-start.4 = (bf16[16,1664]{1,0:T(8,128)(2,1)S(1)}, bf16[16,1664]{1,0:T(8,128)(2,1)S(1)}, u32[]{:S(2)}, u32[]{:S(2)}) collective-permute-start(bf16[16,1664]{1,0:T(8,128)(2,1)S(1)} %pad_maximum_fusion.5), channel_id=1, source_target_pairs={{0,32},{1,33},{2,34},{3,35},{4,36},{5,37},{6,38},{7,39},{8,40},{9,... | collective-permute-start | bytes 159752 | tf_op jit(solution)/shard_map/ppermute | solution.py:42
  9.3 27.0 %collective-permute-start.8 = (bf16[2,2048,128]{2,1,0:T(8,128)(2,1)}, bf16[2,2048,128]{2,1,0:T(8,128)(2,1)S(1)}, u32[]{:S(2)}, u32[]{:S(2)}) collective-permute-start(bf16[2,2048,128]{2,1,0:T(8,128)(2,1)} %get-tuple-element.57), channel_id=1, source_target_pairs={{0,8},{1,9},{2,10},{3,11},{4,12},{5,13},{6,14},{7,15},{8,0},{9,1},... | collective-permute-start | bytes 3145736 | tf_op jit(solution)/shard_map/ppermute | solution.py:42
  10.3 4.3 %collective-permute-start.3 = (bf16[64,512]{1,0:T(8,128)(2,1)S(1)}, bf16[64,512]{1,0:T(8,128)(2,1)S(1)}, u32[]{:S(2)}, u32[]{:S(2)}) collective-permute-start(bf16[64,512]{1,0:T(8,128)(2,1)S(1)} %pad_maximum_fusion.4), channel_id=1, source_target_pairs={{0,6},{1,7},{2,4},{3,5},{4,2},{5,3},{6,0},{7,1},{8,14},{9,15},{10,... | collective-permute-start | bytes 196616 | tf_op jit(solution)/shard_map/ppermute | solution.py:42
  14.7 21.6 %collective-permute-start.9 = (bf16[2,2048,128]{2,1,0:T(8,128)(2,1)}, bf16[2,2048,128]{2,1,0:T(8,128)(2,1)S(1)}, u32[]{:S(2)}, u32[]{:S(2)}) collective-permute-start(bf16[2,2048,128]{2,1,0:T(8,128)(2,1)} %get-tuple-element.58), channel_id=1, source_target_pairs={{0,2},{1,3},{2,4},{3,5},{4,6},{5,7},{6,0},{7,1},{8,10},{9,11},{10,... | collective-permute-start | bytes 3145736 | tf_op jit(solution)/shard_map/ppermute | solution.py:42
  14.8 22.8 %collective-permute-start.10 = (bf16[2,2048,128]{2,1,0:T(8,128)(2,1)}, bf16[2,2048,128]{2,1,0:T(8,128)(2,1)S(1)}, u32[]{:S(2)}, u32[]{:S(2)}) collective-permute-start(bf16[2,2048,128]{2,1,0:T(8,128)(2,1)} %get-tuple-element.59), channel_id=1, source_target_pairs={{0,6},{1,7},{2,0},{3,1},{4,2},{5,3},{6,4},{7,5},{8,14},{9,15},{10,... | collective-permute-start | bytes 3145736 | tf_op jit(solution)/shard_map/ppermute | solution.py:42
  16.2 7.9 %collective-permute-start.6 = (bf16[32,1664]{1,0:T(8,128)(2,1)S(1)}, bf16[32,1664]{1,0:T(8,128)(2,1)S(1)}, u32[]{:S(2)}, u32[]{:S(2)}) collective-permute-start(bf16[32,1664]{1,0:T(8,128)(2,1)S(1)} %pad_maximum_fusion.3), channel_id=1, source_target_pairs={{0,96},{1,97},{2,98},{3,99},{4,100},{5,101},{6,102},{7,103},{8,104... | collective-permute-start | bytes 319496 | tf_op jit(solution)/shard_map/ppermute | solution.py:42
  20.1 5.0 %collective-permute-start.5 = (bf16[64,1024]{1,0:T(8,128)(2,1)S(1)}, bf16[64,1024]{1,0:T(8,128)(2,1)S(1)}, u32[]{:S(2)}, u32[]{:S(2)}) collective-permute-start(bf16[64,1024]{1,0:T(8,128)(2,1)S(1)} %pad_maximum_fusion.2), channel_id=1, source_target_pairs={{0,1},{1,0},{2,3},{3,2},{4,5},{5,4},{6,7},{7,6},{8,9},{9,8},{10,11... | collective-permute-start | bytes 393224 | tf_op jit(solution)/shard_map/ppermute | solution.py:42
  25.8 23.8 %copy-start.12 = (f32[1664]{0:T(1024)S(1)}, f32[1664]{0:T(1024)}, u32[]{:S(2)}) copy-start(f32[1664]{0:T(1024)} %param.8) | copy-start | bytes 19972
  32.4 3.9 %copy-start.13 = (f32[1,1664]{1,0:T(1,128)S(1)}, f32[1,1664]{1,0:T(1,128)}, u32[]{:S(2)}) copy-start(f32[1,1664]{1,0:T(1,128)} %get-tuple-element.56) | copy-start | bytes 19972
  32.4 3.9 %collective-permute-start.7 = (f32[1,1664]{1,0:T(1,128)}, f32[1,1664]{1,0:T(1,128)S(1)}, u32[]{:S(2)}, u32[]{:S(2)}) collective-permute-start(f32[1,1664]{1,0:T(1,128)} %get-tuple-element.56), channel_id=1, source_target_pairs={{0,16},{1,17},{2,18},{3,19},{4,20},{5,21},{6,22},{7,23},{8,24},{9,... | collective-permute-start | bytes 19976 | tf_op jit(solution)/shard_map/ppermute | solution.py:42
  36.3 58.4 %copy-start.4 = (bf16[2,2048,128]{2,1,0:T(8,128)(2,1)}, bf16[2,2048,128]{2,1,0:T(8,128)(2,1)S(1)}, u32[]{:S(2)}) copy-start(bf16[2,2048,128]{2,1,0:T(8,128)(2,1)S(1)} %collective-permute-done.8.refs_2_) | copy-start | bytes 3145732
  36.3 58.4 %copy-start.5 = (bf16[2,2048,128]{2,1,0:T(8,128)(2,1)}, bf16[2,2048,128]{2,1,0:T(8,128)(2,1)S(1)}, u32[]{:S(2)}) copy-start(bf16[2,2048,128]{2,1,0:T(8,128)(2,1)S(1)} %collective-permute-done.9.refs_4_) | copy-start | bytes 3145732
  37.6 55.2 %copy-start.6 = (bf16[2,2048,128]{2,1,0:T(8,128)(2,1)}, bf16[2,2048,128]{2,1,0:T(8,128)(2,1)S(1)}, u32[]{:S(2)}) copy-start(bf16[2,2048,128]{2,1,0:T(8,128)(2,1)S(1)} %collective-permute-done.10.refs_6_) | copy-start | bytes 3145732
  37.6 32.6 %collective-permute-start.13 = (bf16[2,2048,128]{2,1,0:T(8,128)(2,1)}, bf16[2,2048,128]{2,1,0:T(8,128)(2,1)}, u32[]{:S(2)}, u32[]{:S(2)}) collective-permute-start(bf16[2,2048,128]{2,1,0:T(8,128)(2,1)} %get-tuple-element.64), channel_id=1, source_target_pairs={{0,12},{1,13},{2,14},{3,15},{4,8},{5,9},{6,10},{7,11},{8,4},{9,5},... | collective-permute-start | bytes 3145736 | tf_op jit(solution)/shard_map/ppermute | solution.py:42
  40.6 30.1 %collective-permute-start.21 = (bf16[2,2048,128]{2,1,0:T(8,128)(2,1)S(1)}, bf16[2,2048,128]{2,1,0:T(8,128)(2,1)}, u32[]{:S(2)}, u32[]{:S(2)}) collective-permute-start(bf16[2,2048,128]{2,1,0:T(8,128)(2,1)S(1)} %collective-permute-done.8.refs_2_), channel_id=1, source_target_pairs={{0,1},{1,0},{2,3},{3,2},{4,5},{5,4},{6,7},{7,6},{8,9},{9,8},{10,11... | collective-permute-start | bytes 3145736 | tf_op jit(solution)/shard_map/ppermute | solution.py:42
  44.8 2.5 %collective-permute-start.11 = (f32[1,1664]{1,0:T(1,128)S(1)}, f32[1,1664]{1,0:T(1,128)S(1)}, u32[]{:S(2)}, u32[]{:S(2)}) collective-permute-start(f32[1,1664]{1,0:T(1,128)S(1)} %add.9), channel_id=1, source_target_pairs={{0,32},{1,33},{2,34},{3,35},{4,36},{5,37},{6,38},{7,39},{8,40},{9,... | collective-permute-start | bytes 19976 | tf_op jit(solution)/shard_map/ppermute | solution.py:42
  47.3 4.2 %collective-permute-start.12 = (f32[1,1664]{1,0:T(1,128)S(1)}, f32[1,1664]{1,0:T(1,128)S(1)}, u32[]{:S(2)}, u32[]{:S(2)}) collective-permute-start(f32[1,1664]{1,0:T(1,128)S(1)} %add.10), channel_id=1, source_target_pairs={{0,96},{1,97},{2,98},{3,99},{4,100},{5,101},{6,102},{7,103},{8,104... | collective-permute-start | bytes 19976 | tf_op jit(solution)/shard_map/ppermute | solution.py:42
  54.2 16.0 %all-to-all-start = ((bf16[16,80,128]{2,1,0:T(8,128)(2,1)}), bf16[16,80,128]{2,1,0:T(8,128)(2,1)S(1)}, u32[]{:S(2)}, u32[]{:S(2)}) async-start(bf16[16,80,128]{2,1,0:T(8,128)(2,1)} %pack_extras.1), calls=%async_computation | async-start | bytes 655360 | tf_op jit(solution)/shard_map/all_to_all | solution.py:303
  61.5 12.4 %collective-permute-start.22 = (bf16[2,2048,128]{2,1,0:T(8,128)(2,1)S(1)}, bf16[2,2048,128]{2,1,0:T(8,128)(2,1)}, u32[]{:S(2)}, u32[]{:S(2)}) collective-permute-start(bf16[2,2048,128]{2,1,0:T(8,128)(2,1)S(1)} %collective-permute-done.9.refs_4_), channel_id=1, source_target_pairs={{0,1},{1,0},{2,3},{3,2},{4,5},{5,4},{6,7},{7,6},{8,9},{9,8},{10,11... | collective-permute-start | bytes 3145736 | tf_op jit(solution)/shard_map/ppermute | solution.py:42
  61.9 12.7 %collective-permute-start.23 = (bf16[2,2048,128]{2,1,0:T(8,128)(2,1)S(1)}, bf16[2,2048,128]{2,1,0:T(8,128)(2,1)}, u32[]{:S(2)}, u32[]{:S(2)}) collective-permute-start(bf16[2,2048,128]{2,1,0:T(8,128)(2,1)S(1)} %collective-permute-done.10.refs_6_), channel_id=1, source_target_pairs={{0,1},{1,0},{2,3},{3,2},{4,5},{5,4},{6,7},{7,6},{8,9},{9,8},{10,11... | collective-permute-start | bytes 3145736 | tf_op jit(solution)/shard_map/ppermute | solution.py:42
  70.2 24.6 %copy-start = (bf16[16,80,128]{2,1,0:T(8,128)(2,1)}, bf16[16,80,128]{2,1,0:T(8,128)(2,1)S(1)}, u32[]{:S(2)}) copy-start(bf16[16,80,128]{2,1,0:T(8,128)(2,1)S(1)} %all-to-all-done.extras) | copy-start | bytes 983044
  70.2 22.6 %collective-permute-start.20 = (bf16[2,2048,128]{2,1,0:T(8,128)(2,1)}, bf16[2,2048,128]{2,1,0:T(8,128)(2,1)S(1)}, u32[]{:S(2)}, u32[]{:S(2)}) collective-permute-start(bf16[2,2048,128]{2,1,0:T(8,128)(2,1)} %get-tuple-element.80.refs_0_), channel_id=1, source_target_pairs={{0,1},{1,0},{2,3},{3,2},{4,5},{5,4},{6,7},{7,6},{8,9},{9,8},{10,11... | collective-permute-start | bytes 3145736 | tf_op jit(solution)/shard_map/ppermute | solution.py:42
  70.6 23.2 %collective-permute-start.24 = (bf16[2,2048,128]{2,1,0:T(8,128)(2,1)}, bf16[2,2048,128]{2,1,0:T(8,128)(2,1)S(1)}, u32[]{:S(2)}, u32[]{:S(2)}) collective-permute-start(bf16[2,2048,128]{2,1,0:T(8,128)(2,1)} %collective-permute-done.13.refs_8_), channel_id=1, source_target_pairs={{0,1},{1,0},{2,3},{3,2},{4,5},{5,4},{6,7},{7,6},{8,9},{9,8},{10,11... | collective-permute-start | bytes 3145736 | tf_op jit(solution)/shard_map/ppermute | solution.py:42
  70.7 15.9 %collective-permute-start.17 = (bf16[1,2048,128]{2,1,0:T(8,128)(2,1)}, bf16[1,2048,128]{2,1,0:T(8,128)(2,1)S(1)}, u32[]{:S(2)}, u32[]{:S(2)}) collective-permute-start(bf16[1,2048,128]{2,1,0:T(8,128)(2,1)} %get-tuple-element.77), channel_id=1, source_target_pairs={{0,10},{1,11},{2,12},{3,13},{4,14},{5,15},{6,8},{7,9},{8,2},{9,3},... | collective-permute-start | bytes 1572872 | tf_op jit(solution)/shard_map/ppermute | solution.py:42
  73.8 27.1 %collective-permute-start.18 = (bf16[1,2048,128]{2,1,0:T(8,128)(2,1)}, bf16[1,2048,128]{2,1,0:T(8,128)(2,1)}, u32[]{:S(2)}, u32[]{:S(2)}) collective-permute-start(bf16[1,2048,128]{2,1,0:T(8,128)(2,1)} %get-tuple-element.78), channel_id=1, source_target_pairs={{0,14},{1,15},{2,8},{3,9},{4,10},{5,11},{6,12},{7,13},{8,6},{9,7},... | collective-permute-start | bytes 1572872 | tf_op jit(solution)/shard_map/ppermute | solution.py:42
  74.6 26.3 %collective-permute-start.19 = (bf16[1,2048,128]{2,1,0:T(8,128)(2,1)}, bf16[1,2048,128]{2,1,0:T(8,128)(2,1)}, u32[]{:S(2)}, u32[]{:S(2)}) collective-permute-start(bf16[1,2048,128]{2,1,0:T(8,128)(2,1)} %get-tuple-element.79), channel_id=1, source_target_pairs={{0,4},{1,5},{2,6},{3,7},{4,0},{5,1},{6,2},{7,3},{8,12},{9,13},{10,... | collective-permute-start | bytes 1572872 | tf_op jit(solution)/shard_map/ppermute | solution.py:42
  86.6 8.2 %copy-start.9 = (bf16[1,2048,128]{2,1,0:T(8,128)(2,1)}, bf16[1,2048,128]{2,1,0:T(8,128)(2,1)S(1)}, u32[]{:S(2)}) copy-start(bf16[1,2048,128]{2,1,0:T(8,128)(2,1)S(1)} %collective-permute-done.17.refs_0_) | copy-start | bytes 1572868
  86.6 25.1 %collective-permute-start.14 = (bf16[1,2048,128]{2,1,0:T(8,128)(2,1)}, bf16[1,2048,128]{2,1,0:T(8,128)(2,1)S(1)}, u32[]{:S(2)}, u32[]{:S(2)}) collective-permute-start(bf16[1,2048,128]{2,1,0:T(8,128)(2,1)} %get-tuple-element.74), channel_id=1, source_target_pairs={{0,11},{1,10},{2,13},{3,12},{4,15},{5,14},{6,9},{7,8},{8,3},{9,2},... | collective-permute-start | bytes 1572872 | tf_op jit(solution)/shard_map/ppermute | solution.py:42
  92.8 1.0 copy-start.7
  92.8 29.4 %collective-permute-start.15 = (bf16[1,2048,128]{2,1,0:T(8,128)(2,1)}, bf16[1,2048,128]{2,1,0:T(8,128)(2,1)S(1)}, u32[]{:S(2)}, u32[]{:S(2)}) collective-permute-start(bf16[1,2048,128]{2,1,0:T(8,128)(2,1)} %get-tuple-element.75), channel_id=1, source_target_pairs={{0,15},{1,14},{2,9},{3,8},{4,11},{5,10},{6,13},{7,12},{8,7},{9,6},... | collective-permute-start | bytes 1572872 | tf_op jit(solution)/shard_map/ppermute | solution.py:42
  93.8 1.0 copy-start.8
  94.7 28.9 %collective-permute-start.16 = (bf16[1,2048,128]{2,1,0:T(8,128)(2,1)}, bf16[1,2048,128]{2,1,0:T(8,128)(2,1)S(1)}, u32[]{:S(2)}, u32[]{:S(2)}) collective-permute-start(bf16[1,2048,128]{2,1,0:T(8,128)(2,1)} %get-tuple-element.76), channel_id=1, source_target_pairs={{0,5},{1,4},{2,7},{3,6},{4,1},{5,0},{6,3},{7,2},{8,13},{9,12},{10,... | collective-permute-start | bytes 1572872 | tf_op jit(solution)/shard_map/ppermute | solution.py:42
  100.9 22.8 %copy-start.1 = (bf16[16,80,128]{2,1,0:T(8,128)(2,1)S(1)}, bf16[16,80,128]{2,1,0:T(8,128)(2,1)}, u32[]{:S(2)}) copy-start(bf16[16,80,128]{2,1,0:T(8,128)(2,1)} %copy-done) | copy-start | bytes 983044
  100.9 22.8 %copy-start.2 = (bf16[2048,64]{1,0:T(8,128)(2,1)S(1)}, bf16[2048,64]{1,0:T(8,128)(2,1)}, u32[]{:S(2)}) copy-start(bf16[2048,64]{1,0:T(8,128)(2,1)} %get-tuple-element.54.a) | copy-start | bytes 786436
  100.9 22.8 %copy-start.3 = (s32[16,13]{1,0:T(8,128)S(1)}, s32[16,13]{1,0:T(8,128)}, u32[]{:S(2)}) copy-start(s32[16,13]{1,0:T(8,128)} %tcb.13) | copy-start | bytes 2500
